TPU v7x, 32 devices: a whole 2x2x4 slice. The times are simulated.
32 devices in a mesh: frames: 2 (over y), bricks: 16 (over z, x, core).
Axes of the slice: x: 2, y: 2, z: 4, core: 2. Of those that a mesh axis runs over, the one named last changes fastest.
Arguments:
- recording: bfloat16 [32, 64, 16, 256], P('frames', 'bricks'), may hold values from -1 to 2
- traces: bfloat16 [32, 512], P('frames', 'bricks'), may hold values from 0 to 2
- footprints: bfloat16 [512, 16384], P('bricks'), may hold values from 0 to 1, as said below
- block_owner: int32 [512, 1], P('bricks'), may hold values from 0 to 15; in each aligned block of 32 rows (0 to 31, 32 to 63, ...) at most 4 rows name the same one
- block_slot: int32 [512], P('bricks'), may hold values from 0 to 31
Outputs:
- traces_new: float32 [32, 512], P('frames', 'bricks')
- footprints_new: bfloat16 [512, 16384], P('bricks')
Inputs may be any that keep to these rules, and one draw needn't show every extreme that they name: `footprints`: each row is positive on exactly 128 voxels forming a run in the slab's flat voxel order taken circularly, and 0 elsewhere; positive entries are at least 0.02. `block_owner`: among the 32 blocks of one slab, at most 4 have the same owner.
All inputs are finite; a program needn't handle non-finite values.
Results may differ from a plain program's by a relative error of at most 0.0033.
Values may be sent and summed in bfloat16 or wider, within the bound.
A program may use at most 64 MiB of HBM per device.

v0:
```python
import jax
import jax.numpy as jnp
from jax import lax
from jax.sharding import PartitionSpec as P

SEND_CAP = 4


TIME_STEP = 0.14
EDGE_SCALE = 1.0
HIGHEST = lax.Precision.HIGHEST


def padded_2(cells, sides, width):
    for axis, dim in sides:
        count = lax.axis_size(axis)
        ends = count - 1
        head = lax.slice_in_dim(cells, 0, width, axis=dim)
        tail = lax.slice_in_dim(cells, cells.shape[dim] - width, cells.shape[dim], axis=dim)
        cells = jnp.concatenate(
            [
                lax.ppermute(tail, axis, [(i, (i + 1) % count) for i in range(ends)]),
                cells,
                lax.ppermute(head, axis, [((i + 1) % count, i) for i in range(ends)]),
            ],
            axis=dim,
        )
    return cells


def edge_flux(center, other):
    difference = other - center
    return difference / (1.0 + (difference / EDGE_SCALE) ** 2)


def relax_once(extended):
    center = extended[:, 1:-1]
    padded = jnp.pad(center, ((0, 0), (0, 0), (1, 1), (1, 1)))
    summed_flux = edge_flux(center, extended[:, 2:]) + edge_flux(center, extended[:, :-2])
    summed_flux = (
        summed_flux
        + edge_flux(center, padded[:, :, 2:, 1:-1])
        + edge_flux(center, padded[:, :, :-2, 1:-1])
    )
    summed_flux = (
        summed_flux
        + edge_flux(center, padded[:, :, 1:-1, 2:])
        + edge_flux(center, padded[:, :, 1:-1, :-2])
    )
    return center + TIME_STEP * summed_flux


def denoise(recording):
    current = recording.astype(jnp.float32)
    for sweep in range(3):
        extended = padded_2(current, (("bricks", 1),), 1)
        current = relax_once(extended)
    return current


def contract_first(left, right, precision=None):
    return lax.dot_general(
        left,
        right,
        (((0,), (0,)), ((), ())),
        precision=precision,
        preferred_element_type=jnp.float32,
    )


def finish_rows(foot_rows, product_rows, gram_rows, diag_rows, foot_all):
    current = foot_rows.astype(jnp.float32)
    gradient = product_rows - jnp.dot(gram_rows, foot_all.astype(jnp.float32), precision=HIGHEST)
    stepped = jnp.where(
        current > 0, jnp.maximum(current + gradient / (diag_rows + 1.0)[:, None], 0.0), 0.0
    )
    return stepped.astype(jnp.bfloat16)


def shards(recording, traces, footprints, block_owner, block_slot):
    frame_count = recording.shape[0]
    slots = footprints.shape[0]
    voxels = footprints.shape[1]
    owned = traces.shape[1]
    n_bricks = lax.axis_size("bricks")
    all_comps = owned * n_bricks
    denoised = denoise(recording).astype(jnp.bfloat16).reshape(frame_count, voxels)
    owner = block_owner[:, 0]
    component = owner * owned + block_slot
    selector = (component[None, :] == jnp.arange(all_comps, dtype=jnp.int32)[:, None]).astype(
        jnp.bfloat16
    )
    all_prior = lax.all_gather(traces, "bricks", axis=1, tiled=True)
    slot_traces = jnp.dot(all_prior, selector, preferred_element_type=jnp.float32)
    correlation = lax.dot_general(
        footprints, footprints, (((1,), (1,)), ((), ())), preferred_element_type=jnp.float32
    )
    projected = lax.dot_general(
        denoised, footprints, (((1,), (1,)), ((), ())), preferred_element_type=jnp.float32
    )
    partial_value = projected - jnp.dot(slot_traces, correlation, precision=HIGHEST)
    diag_part = jnp.diagonal(correlation)
    shared = owner[:, None] == owner[None, :]
    earlier = jnp.arange(slots)[:, None] > jnp.arange(slots)[None, :]
    position = jnp.sum((shared & earlier).astype(jnp.int32), axis=1)
    target = owner * SEND_CAP + position
    place = (target[:, None] == jnp.arange(n_bricks * SEND_CAP, dtype=jnp.int32)[None, :]).astype(
        jnp.float32
    )
    send_vals = contract_first(place, partial_value.T, HIGHEST).reshape(
        n_bricks, SEND_CAP, frame_count
    )
    send_diag = jnp.dot(diag_part, place, precision=HIGHEST).reshape(n_bricks, SEND_CAP)
    send_ids = jnp.dot((block_slot + 1).astype(jnp.float32), place, precision=HIGHEST).reshape(
        n_bricks, SEND_CAP
    )
    recv_vals, recv_diag, recv_ids = (
        lax.all_to_all(send_vals, "bricks", split_axis=0, concat_axis=0, tiled=True),
        lax.all_to_all(send_diag, "bricks", split_axis=0, concat_axis=0, tiled=True),
        lax.all_to_all(send_ids, "bricks", split_axis=0, concat_axis=0, tiled=True),
    )
    take = (
        recv_ids.reshape(-1)[:, None]
        == (jnp.arange(owned, dtype=jnp.int32) + 1).astype(jnp.float32)[None, :]
    ).astype(jnp.float32)
    summed = contract_first(recv_vals.reshape(n_bricks * SEND_CAP, frame_count), take, HIGHEST)
    diag_sum = jnp.dot(recv_diag.reshape(1, -1), take, precision=HIGHEST)
    traces_new = jnp.maximum(0.0, traces.astype(jnp.float32) + summed / (diag_sum + 1.0))
    new_bf = traces_new.astype(jnp.bfloat16)
    reply = lax.dot_general(
        take.astype(jnp.bfloat16),
        new_bf,
        (((1,), (1,)), ((), ())),
        preferred_element_type=jnp.float32,
    )
    reply = reply.astype(jnp.bfloat16).reshape(n_bricks, SEND_CAP, frame_count)
    returned = lax.all_to_all(reply, "bricks", split_axis=0, concat_axis=0, tiled=True)
    slot_new = lax.dot_general(
        returned.reshape(n_bricks * SEND_CAP, frame_count),
        place.astype(jnp.bfloat16),
        (((0,), (1,)), ((), ())),
        preferred_element_type=jnp.float32,
    )
    new_slots_bf = slot_new.astype(jnp.bfloat16)
    gram_part = contract_first(slot_new, slot_new, HIGHEST)
    product_part = contract_first(new_slots_bf, denoised)
    product, gram = lax.psum((product_part, gram_part), "frames")
    footprints_new = finish_rows(footprints, product, gram, jnp.diagonal(gram), footprints)
    return (traces_new, footprints_new)


def solution(mesh):
    return jax.shard_map(
        shards,
        mesh=mesh,
        in_specs=(
            P("frames", "bricks", None, None),
            P("frames", "bricks"),
            P("bricks", None),
            P("bricks", None),
            P("bricks"),
        ),
        out_specs=(P("frames", "bricks"), P("bricks", None)),
        check_vma=False,
    )
```

profile of v0, /device:TPU:0, one launch (start us, length us, event | category | flops | bytes accessed | tf_op | source)
XLA Modules:
  0.0 166.7 jit_solution(14490374163330252274)
XLA Ops:
  7.2 0.0 copy-start.1
  7.2 0.0 copy-start.3
  7.2 1.1 fusion.51
  8.3 1.3 collective-permute-start
  9.6 3.0 %collective-permute-start.1 = (f32[16,1,16,256]{3,2,1,0:T(8,128)S(1)}, f32[16,1,16,256]{3,2,1,0:T(8,128)S(1)}, u32[]{:S(2)}, u32[]{:S(2)}) collective-permute-start(f32[16,1,16,256]{3,2,1,0:T(8,128)S(1)} %get-tuple-element.7), channel_id=1, source_target_pairs={{0,1},{1,2},{2,3},{3,4},{4,5},{5,6},{6,7},{7,8},{8,9},{9,10},{10,1... | collective-permute-start | bytes 786440 | tf_op jit(solution)/shard_map/ppermute | solution.py:22
  12.6 2.0 %fusion.52 = f32[32,32]{1,0:T(8,128)S(1)} fusion(bf16[32,16384]{1,0:T(8,128)(2,1)} %param.7), kind=kOutput, calls=%fused_computation.99 | convolution fusion | flops 33554432 | bytes 1052672 | tf_op jit(solution)/shard_map/dot_general | solution.py:95
  14.6 0.0 copy-done.3
  14.6 0.2 convert_reduce_fusion
  14.8 0.7 gather_fusion
  15.5 0.2 convolution_bitcast_fusion.1
  15.7 0.7 all_to_all.21
  16.4 7.9 %all-to-all-start.2 = ((f32[16,1,4]{2,1,0:T(1,128)}), f32[16,1,4]{2,1,0:T(1,128)S(1)}, u32[]{:S(2)}, u32[]{:S(2)}) async-start(f32[16,1,4]{2,1,0:T(1,128)} %bitcast.13), calls=%async_computation.2 | async-start | bytes 16384 | tf_op jit(solution)/shard_map/all_to_all | solution.py:119
  24.3 0.1 convert_element_type.57
  24.5 0.0 copy-start.4
  24.5 0.0 copy-start.2
  24.5 0.0 collective-permute-done
  24.5 0.0 collective-permute-done.1
  24.5 1.7 convert_add_fusion
  26.2 1.3 collective-permute-start.2
  27.5 3.0 %collective-permute-start.3 = (f32[16,1,16,256]{3,2,1,0:T(8,128)S(1)}, f32[16,1,16,256]{3,2,1,0:T(8,128)S(1)}, u32[]{:S(2)}, u32[]{:S(2)}) collective-permute-start(f32[16,1,16,256]{3,2,1,0:T(8,128)S(1)} %get-tuple-element.5), channel_id=1, source_target_pairs={{0,1},{1,2},{2,3},{3,4},{4,5},{5,6},{6,7},{7,8},{8,9},{9,10},{10,1... | collective-permute-start | bytes 786440 | tf_op jit(solution)/shard_map/ppermute | solution.py:22
  30.6 0.0 copy-done.2
  30.6 21.9 %all-gather = bf16[16,32,16]{1,2,0:T(8,128)(2,1)S(1)} all-gather(bf16[1,32,16]{1,2,0:T(8,128)(2,1)S(1)} %bitcast.60), channel_id=1, replica_groups=mesh['frames'=2,'bricks'=16] {'bricks'}, dimensions={0}, use_global_device_ids=true | all-gather | bytes 17408 | tf_op jit(solution)/shard_map/all_gather | solution.py:93
  52.5 0.1 reshape.68
  52.6 0.2 fusion.20
  52.8 0.0 collective-permute-done.2
  52.8 0.0 collective-permute-done.3
  52.8 1.6 multiply_add_fusion
  54.4 0.0 copy-start
  54.5 1.4 collective-permute-start.4
  55.9 3.0 %collective-permute-start.5 = (f32[16,1,16,256]{3,2,1,0:T(8,128)S(1)}, f32[16,1,16,256]{3,2,1,0:T(8,128)S(1)}, u32[]{:S(2)}, u32[]{:S(2)}) collective-permute-start(f32[16,1,16,256]{3,2,1,0:T(8,128)S(1)} %get-tuple-element.3), channel_id=1, source_target_pairs={{0,1},{1,2},{2,3},{3,4},{4,5},{5,6},{6,7},{7,8},{8,9},{9,10},{10,1... | collective-permute-start | bytes 786440 | tf_op jit(solution)/shard_map/ppermute | solution.py:22
  59.0 0.1 fusion.53
  59.1 0.2 convolution_bitcast_fusion.2
  59.3 0.7 all_to_all.19
  60.0 0.0 all-to-all-done.2
  60.0 3.5 %all-to-all-start.1 = ((f32[16,1,4]{2,1,0:T(1,128)}), f32[16,1,4]{2,1,0:T(1,128)S(1)}, u32[]{:S(2)}, u32[]{:S(2)}) async-start(f32[16,1,4]{2,1,0:T(1,128)} %bitcast.9), calls=%async_computation.1 | async-start | bytes 16384 | tf_op jit(solution)/shard_map/all_to_all | solution.py:120
  63.5 0.5 broadcast.88
  64.0 0.7 reduce.7
  64.7 0.1 reshape.73
  64.8 5.0 %all-to-all-done.1 = f32[16,1,4]{2,1,0:T(1,128)S(1)} async-done(((f32[16,1,4]{2,1,0:T(1,128)}), f32[16,1,4]{2,1,0:T(1,128)S(1)}, u32[]{:S(2)}, u32[]{:S(2)}) %all-to-all-start.1) | async-done | bytes 288 | tf_op jit(solution)/shard_map/all_to_all | solution.py:120
  69.8 0.7 reduce.6
  70.5 0.1 eq.69
  70.6 0.0 collective-permute-done.4
  70.6 0.0 collective-permute-done.5
  70.6 1.6 add_convert_fusion
  72.2 0.3 copy.21
  72.5 0.4 convolution_subtract_fusion.1
  72.9 0.9 fusion.34
  73.8 3.5 %all-to-all-start = ((f32[16,4,16]{2,1,0:T(4,128)}), f32[16,4,16]{2,1,0:T(4,128)S(1)}, u32[]{:S(2)}, u32[]{:S(2)}) async-start(f32[16,4,16]{2,1,0:T(4,128)} %bitcast.5), calls=%async_computation | async-start | bytes 65536 | tf_op jit(solution)/shard_map/all_to_all | solution.py:118
  77.4 0.0 all-reduce.5.cloned.1.call-start
  77.4 0.2 fusion.7
  77.6 6.4 %all-to-all-done = f32[16,4,16]{2,1,0:T(4,128)S(1)} async-done(((f32[16,4,16]{2,1,0:T(4,128)}), f32[16,4,16]{2,1,0:T(4,128)S(1)}, u32[]{:S(2)}, u32[]{:S(2)}) %all-to-all-start) | async-done | bytes 4128 | tf_op jit(solution)/shard_map/all_to_all | solution.py:118
  83.9 0.2 fusion.6
  84.2 0.0 copy-start.5
  84.2 0.2 convolution_convert_fusion
  84.4 0.1 copy.19
  84.5 9.1 %all_to_all.28 = bf16[16,4,16]{2,1,0:T(4,128)(2,1)S(1)} all-to-all(bf16[16,4,16]{2,1,0:T(4,128)(2,1)S(1)} %bitcast.57), channel_id=1, replica_groups=mesh['frames'=2,'bricks'=16] {'bricks'}, dimensions={0} | all-to-all | bytes 4096 | tf_op jit(solution)/shard_map/all_to_all | solution.py:137
  93.5 0.2 fusion.36
  93.7 1.8 %fusion.41 = f32[32,16384]{1,0:T(8,128)} fusion(bf16[16,16384]{1,0:T(8,128)(2,1)S(1)} %bitcast.55, f32[16,32]{1,0:T(8,128)S(1)} %fusion.36), kind=kOutput, calls=%fused_computation.82 | convolution fusion | flops 16777728 | bytes 2623488 | tf_op jit(solution)/shard_map/dot_general | solution.py:62
  95.5 0.0 all-reduce.5.cloned.1.call-update
  95.6 0.2 fusion.54
  95.8 8.5 %psum.15 = f32[32,32]{1,0:T(8,128)S(1)} all-reduce(f32[32,32]{1,0:T(8,128)S(1)} %fusion.54), channel_id=1, replica_groups=mesh['frames'=2,'bricks'=16] {'frames'}, use_global_device_ids=true, to_apply=%region_2.3 | all-reduce | flops 1024 | bytes 8192 | tf_op jit(solution)/shard_map/psum | solution.py:147
  104.2 0.7 gather_fusion.1
  105.0 51.0 %all-reduce.5.cloned.1.call-done = f32[32,16384]{1,0:T(8,128)} async-done(((f32[32,16384]{1,0:T(8,128)}), f32[32,16384]{1,0:T(8,128)}) %all-reduce.5.cloned.1.call-update) | async-done | bytes 2097168 | tf_op jit(solution)/shard_map/psum | solution.py:147
  155.9 4.0 %fusion.4 = bf16[32,16384]{1,0:T(8,128)(2,1)} fusion(f32[32,16384]{1,0:T(8,128)} %all-reduce.5.cloned.1.call-done, f32[32,32]{1,0:T(8,128)S(1)} %psum.15, bf16[32,16384]{1,0:T(8,128)(2,1)S(1)} %copy-done, f32[32]{0:T(128)S(1)} %broadcast_add_fusion), kind=kOutput, calls=%fused_computation.7 | convolution fusion | flops 205520896 | bytes 4198528 | tf_op jit(solution)/shard_map/dot_general | solution.py:73
  (12 shorter events, 0.1 us)
Async XLA Ops:
  7.2 17.2 %copy-start.1 = (bf16[16,4,16,256]{3,2,1,0:T(8,128)(2,1)S(1)}, bf16[16,4,16,256]{3,2,1,0:T(8,128)(2,1)}, u32[]{:S(2)}) copy-start(bf16[16,4,16,256]{3,2,1,0:T(8,128)(2,1)} %param.5) | copy-start | bytes 1572868
  7.2 7.4 %copy-start.3 = (s32[32,1]{0,1:T(1,128)S(1)}, s32[32,1]{0,1:T(1,128)}, u32[]{:S(2)}) copy-start(s32[32,1]{0,1:T(1,128)} %param.8) | copy-start | bytes 388
  8.3 16.2 %collective-permute-start = (f32[16,1,16,256]{3,2,1,0:T(8,128)S(1)}, f32[16,1,16,256]{3,2,1,0:T(8,128)S(1)}, u32[]{:S(2)}, u32[]{:S(2)}) collective-permute-start(f32[16,1,16,256]{3,2,1,0:T(8,128)S(1)} %get-tuple-element.6), channel_id=1, source_target_pairs={{1,0},{2,1},{3,2},{4,3},{5,4},{6,5},{7,6},{8,7},{9,8},{10,9},{11,1... | collective-permute-start | bytes 786440 | tf_op jit(solution)/shard_map/ppermute | solution.py:24
  9.6 14.9 %collective-permute-start.1 = (f32[16,1,16,256]{3,2,1,0:T(8,128)S(1)}, f32[16,1,16,256]{3,2,1,0:T(8,128)S(1)}, u32[]{:S(2)}, u32[]{:S(2)}) collective-permute-start(f32[16,1,16,256]{3,2,1,0:T(8,128)S(1)} %get-tuple-element.7), channel_id=1, source_target_pairs={{0,1},{1,2},{2,3},{3,4},{4,5},{5,6},{6,7},{7,8},{8,9},{9,10},{10,1... | collective-permute-start | bytes 786440 | tf_op jit(solution)/shard_map/ppermute | solution.py:22
  16.4 43.6 %all-to-all-start.2 = ((f32[16,1,4]{2,1,0:T(1,128)}), f32[16,1,4]{2,1,0:T(1,128)S(1)}, u32[]{:S(2)}, u32[]{:S(2)}) async-start(f32[16,1,4]{2,1,0:T(1,128)} %bitcast.13), calls=%async_computation.2 | async-start | bytes 16384 | tf_op jit(solution)/shard_map/all_to_all | solution.py:119
  24.5 6.1 %copy-start.4 = (s32[32]{0:T(128)S(1)}, s32[32]{0:T(128)}, u32[]{:S(2)}) copy-start(s32[32]{0:T(128)} %param.9) | copy-start | bytes 388
  24.5 6.1 %copy-start.2 = (bf16[16,32]{1,0:T(8,128)(2,1)S(1)}, bf16[16,32]{1,0:T(8,128)(2,1)}, u32[]{:S(2)}) copy-start(bf16[16,32]{1,0:T(8,128)(2,1)} %param.6) | copy-start | bytes 3076
  26.2 26.6 %collective-permute-start.2 = (f32[16,1,16,256]{3,2,1,0:T(8,128)S(1)}, f32[16,1,16,256]{3,2,1,0:T(8,128)S(1)}, u32[]{:S(2)}, u32[]{:S(2)}) collective-permute-start(f32[16,1,16,256]{3,2,1,0:T(8,128)S(1)} %get-tuple-element.4), channel_id=1, source_target_pairs={{1,0},{2,1},{3,2},{4,3},{5,4},{6,5},{7,6},{8,7},{9,8},{10,9},{11,1... | collective-permute-start | bytes 786440 | tf_op jit(solution)/shard_map/ppermute | solution.py:24
  27.5 25.3 %collective-permute-start.3 = (f32[16,1,16,256]{3,2,1,0:T(8,128)S(1)}, f32[16,1,16,256]{3,2,1,0:T(8,128)S(1)}, u32[]{:S(2)}, u32[]{:S(2)}) collective-permute-start(f32[16,1,16,256]{3,2,1,0:T(8,128)S(1)} %get-tuple-element.5), channel_id=1, source_target_pairs={{0,1},{1,2},{2,3},{3,4},{4,5},{5,6},{6,7},{7,8},{8,9},{9,10},{10,1... | collective-permute-start | bytes 786440 | tf_op jit(solution)/shard_map/ppermute | solution.py:22
  54.4 18.1 %copy-start = (bf16[32,16384]{1,0:T(8,128)(2,1)S(1)}, bf16[32,16384]{1,0:T(8,128)(2,1)}, u32[]{:S(2)}) copy-start(bf16[32,16384]{1,0:T(8,128)(2,1)} %param.7) | copy-start | bytes 3145732
  54.5 16.1 %collective-permute-start.4 = (f32[16,1,16,256]{3,2,1,0:T(8,128)S(1)}, f32[16,1,16,256]{3,2,1,0:T(8,128)S(1)}, u32[]{:S(2)}, u32[]{:S(2)}) collective-permute-start(f32[16,1,16,256]{3,2,1,0:T(8,128)S(1)} %get-tuple-element.2), channel_id=1, source_target_pairs={{1,0},{2,1},{3,2},{4,3},{5,4},{6,5},{7,6},{8,7},{9,8},{10,9},{11,1... | collective-permute-start | bytes 786440 | tf_op jit(solution)/shard_map/ppermute | solution.py:24
  55.9 14.6 %collective-permute-start.5 = (f32[16,1,16,256]{3,2,1,0:T(8,128)S(1)}, f32[16,1,16,256]{3,2,1,0:T(8,128)S(1)}, u32[]{:S(2)}, u32[]{:S(2)}) collective-permute-start(f32[16,1,16,256]{3,2,1,0:T(8,128)S(1)} %get-tuple-element.3), channel_id=1, source_target_pairs={{0,1},{1,2},{2,3},{3,4},{4,5},{5,6},{6,7},{7,8},{8,9},{9,10},{10,1... | collective-permute-start | bytes 786440 | tf_op jit(solution)/shard_map/ppermute | solution.py:22
  60.0 9.8 %all-to-all-start.1 = ((f32[16,1,4]{2,1,0:T(1,128)}), f32[16,1,4]{2,1,0:T(1,128)S(1)}, u32[]{:S(2)}, u32[]{:S(2)}) async-start(f32[16,1,4]{2,1,0:T(1,128)} %bitcast.9), calls=%async_computation.1 | async-start | bytes 16384 | tf_op jit(solution)/shard_map/all_to_all | solution.py:120
  73.8 10.1 %all-to-all-start = ((f32[16,4,16]{2,1,0:T(4,128)}), f32[16,4,16]{2,1,0:T(4,128)S(1)}, u32[]{:S(2)}, u32[]{:S(2)}) async-start(f32[16,4,16]{2,1,0:T(4,128)} %bitcast.5), calls=%async_computation | async-start | bytes 65536 | tf_op jit(solution)/shard_map/all_to_all | solution.py:118
  77.4 78.6 %all-reduce.5.cloned.1.call-start = ((), (), s32[]{:S(2)}) async-start(), calls=%async_computation.4 | async-start | bytes 4194304 | tf_op jit(solution)/shard_map/psum | solution.py:147
  84.2 11.4 %copy-start.5 = (f32[16,32]{1,0:T(8,128)}, f32[16,32]{1,0:T(8,128)S(1)}, u32[]{:S(2)}) copy-start(f32[16,32]{1,0:T(8,128)S(1)} %fusion.6) | copy-start | bytes 6148
Sparse Core Ops, SparseCore 0:
  95.7 60.2 all-reduce.4
where the time goes:
time: 167 us
  waiting for transfers between devices  62.4 us (37%)
  blocking collectives  39.4 us (24%)
  starting transfers between devices  28.1 us (17%)
  between operations  14.4 us (9%)
  matrix products  10.7 us (6%)
  other arithmetic  6.58 us (4%)
  local copies, waits for them, and re-layouts  5.24 us (3%)
    psum x1, waiting for transfers between devices, shards(): product, gram = lax.psum((product_part, gram_part), 'frames')  51 us
    all_gather x1, blocking collectives, shards(): all_prior = lax.all_gather(traces, 'bricks', axis=1, tiled=True)  21.9 us
    ppermute x3, starting transfers between devices, padded_2(): lax.ppermute(tail, axis, [(i, (i + 1) % count) for i in range(ends)])  9.14 us
    all_to_all x1, blocking collectives, shards(): lax.all_to_all(reply, 'bricks', split_axis=0, concat_axis=0, tiled=True)  9.07 us
    psum x1, blocking collectives, shards(): product, gram = lax.psum((product_part, gram_part), 'frames')  8.47 us
    all_to_all x1, starting transfers between devices, shards(): lax.all_to_all(send_diag, 'bricks', split_axis=0, concat_axis=0, tiled=True)  7.91 us
    all_to_all x1, waiting for transfers between devices, shards(): lax.all_to_all(send_vals, 'bricks', split_axis=0, concat_axis=0, tiled=True)  6.35 us
    all_to_all x1, waiting for transfers between devices, shards(): lax.all_to_all(send_ids, 'bricks', split_axis=0, concat_axis=0, tiled=True)  5.01 us
  transfers between devices with their start and end apart: 10, of which 3 were waited for; matrix products, arithmetic and copies ran while one was open for 6% of the time, Pallas kernels for 0%

commit v1 on v0

v1 whole, which is shorter than its diff:
```python
import functools

import jax
import jax.numpy as jnp
from jax import lax
from jax.experimental import pallas as pl
from jax.experimental.pallas import tpu as pltpu
from jax.sharding import PartitionSpec as P

TIME_STEP = 0.14
SWEEPS = 3
LANES = 128
HIGHEST = lax.Precision.HIGHEST
MESH = pl.DeviceIdType.MESH
VMEM = pl.BlockSpec(memory_space=pltpu.VMEM)
SMEM = pl.BlockSpec(memory_space=pltpu.SMEM)


def meet(axes):
    barrier = pltpu.get_barrier_semaphore()
    total = 0
    for axis in axes:
        count = lax.axis_size(axis)
        me = lax.axis_index(axis)

        def tell(d, carry, axis=axis, count=count, me=me):
            pl.semaphore_signal(
                barrier, inc=1, device_id={axis: lax.rem(me + d, count)}, device_id_type=MESH
            )
            return carry

        lax.fori_loop(1, count, tell, 0)
        total += count - 1
    pl.semaphore_wait(barrier, total)


def share_copy(axis, gathered, source, send, recv, d):
    count = lax.axis_size(axis)
    me = lax.axis_index(axis)
    return pltpu.make_async_remote_copy(
        src_ref=source,
        dst_ref=gathered.at[me],
        send_sem=send.at[d],
        recv_sem=recv.at[d],
        device_id={axis: lax.rem(me + d, count)},
        device_id_type=MESH,
    )


def share_start(axis, gathered, source, send, recv):
    def go(d, carry):
        share_copy(axis, gathered, source, send, recv, d).start()
        return carry

    lax.fori_loop(1, lax.axis_size(axis), go, 0)


def share_wait(axis, gathered, source, send, recv):
    def go(d, carry):
        share_copy(axis, gathered, source, send, recv, d).wait()
        return carry

    lax.fori_loop(1, lax.axis_size(axis), go, 0)


def first_exchange(rec, info, low, high, infos, hsend, hrecv, send, recv):
    n = lax.axis_size("bricks")
    me = lax.axis_index("bricks")
    planes = rec.shape[0]
    meet(("bricks",))
    to_right = pltpu.make_async_remote_copy(
        src_ref=rec.at[pl.ds(planes - SWEEPS, SWEEPS)],
        dst_ref=low,
        send_sem=hsend.at[0],
        recv_sem=hrecv.at[0],
        device_id={"bricks": lax.rem(me + 1, n)},
        device_id_type=MESH,
    )
    to_left = pltpu.make_async_remote_copy(
        src_ref=rec.at[pl.ds(0, SWEEPS)],
        dst_ref=high,
        send_sem=hsend.at[1],
        recv_sem=hrecv.at[1],
        device_id={"bricks": lax.rem(me + n - 1, n)},
        device_id_type=MESH,
    )

    @pl.when(me < n - 1)
    def _():
        to_right.start()

    @pl.when(me > 0)
    def _():
        to_left.start()

    share_start("bricks", infos, info, send, recv)
    infos[me] = info[...]

    @pl.when(me == 0)
    def _():
        low[...] = jnp.zeros_like(low)

    @pl.when(me == n - 1)
    def _():
        high[...] = jnp.zeros_like(high)

    share_wait("bricks", infos, info, send, recv)

    @pl.when(me < n - 1)
    def _():
        to_right.wait_send()
        to_left.wait_recv()

    @pl.when(me > 0)
    def _():
        to_left.wait_send()
        to_right.wait_recv()


def flux_of(difference):
    below = 1.0 + difference * difference
    near = pl.reciprocal(below, approx=True)
    return difference * (near * (2.0 - below * near))


def sweep(load, store, planes, rows, shape):
    lane = lax.broadcasted_iota(jnp.int32, shape, 1)
    width = shape[1]

    def row(z, fluxes):
        out = []
        center = load(1, z)
        flux_x = flux_of(center - load(0, z))
        for x in range(planes):
            right = load(x + 2, z)
            next_x = flux_of(right - center)
            ahead = load(x + 1, jnp.minimum(z + 1, rows - 1))
            ahead = jnp.where(z + 1 < rows, ahead, 0.0)
            next_z = flux_of(ahead - center)
            beside = jnp.where(lane == width - 1, 0.0, pltpu.roll(center, width - 1, 1))
            next_y = flux_of(beside - center)
            edge = flux_of(center[:, :LANES])
            edge = jnp.concatenate([edge, jnp.zeros((shape[0], width - LANES), jnp.float32)], axis=1)
            prev_y = jnp.where(lane == 0, edge, pltpu.roll(next_y, 1, 1))
            total = (next_x - flux_x) + (next_z - fluxes[x]) + (next_y - prev_y)
            store(x, z, center + TIME_STEP * total)
            out.append(next_z)
            flux_x = next_x
            center = right
        return tuple(out)

    first = tuple(flux_of(load(x + 1, 0)) for x in range(planes))
    lax.fori_loop(0, rows, row, first)


def local_kernel(
    tiles, at, rec, low, high, foot, slot_traces, message, windows, own, one, two, y_tiles, zero
):
    n = lax.axis_size("bricks")
    me = lax.axis_index("bricks")
    planes, rows, frames, width = rec.shape
    slots = foot.shape[0]
    shape = (frames, width)
    per = width // LANES

    def load_first(x, z):
        if x < SWEEPS:
            return low[x, z].astype(jnp.float32)
        if x < SWEEPS + planes:
            return rec[x - SWEEPS, z].astype(jnp.float32)
        return high[x - SWEEPS - planes, z].astype(jnp.float32)

    def keep(ref, margin):
        def store(x, z, value):
            if x < margin:
                value = jnp.where(me > 0, value, 0.0)
            if x >= planes + margin:
                value = jnp.where(me < n - 1, value, 0.0)
            ref[x, z] = value

        return store

    def store_last(x, z, value):
        value = value.astype(jnp.bfloat16)
        for h in range(per):
            y_tiles[(x * rows + z) * per + h] = value[:, h * LANES : (h + 1) * LANES]

    sweep(load_first, keep(one, 2), planes + 4, rows, shape)
    sweep(lambda x, z: one[x, z], keep(two, 1), planes + 2, rows, shape)
    sweep(lambda x, z: two[x, z], store_last, planes, rows, shape)

    sub = lax.broadcasted_iota(jnp.int32, (slots, 2 * LANES), 0)
    mine = jnp.zeros((slots, 2 * LANES), jnp.float32)
    for k in range(slots):
        t = at[k]
        u = lax.rem(t + 1, tiles)
        rows_a = jnp.concatenate(
            [
                foot[:, pl.ds(pl.multiple_of(t * LANES, LANES), LANES)],
                foot[:, pl.ds(pl.multiple_of(u * LANES, LANES), LANES)],
            ],
            axis=1,
        )
        windows[k, frames:, :] = rows_a
        windows[k, :frames, :] = jnp.concatenate([y_tiles[t], y_tiles[u]], axis=1)
        mine = jnp.where(sub == k, rows_a.astype(jnp.float32), mine)
    own[...] = mine
    mine_bf = mine.astype(jnp.bfloat16)
    wide = frames + slots
    sub = lax.broadcasted_iota(jnp.int32, (slots, wide), 0)
    both = jnp.zeros((slots, wide), jnp.float32)
    for k in range(slots):
        found = lax.dot_general(
            mine_bf, windows[k], (((1,), (1,)), ((), ())), preferred_element_type=jnp.float32
        )
        both = jnp.where(sub == k, found, both)
    correlation = both[:, frames:]
    removed = jnp.dot(correlation, slot_traces[...], precision=HIGHEST)
    eye = lax.broadcasted_iota(jnp.int32, (slots, slots), 0) == lax.broadcasted_iota(
        jnp.int32, (slots, slots), 1
    )
    diag = jnp.sum(jnp.where(eye, correlation, 0.0), axis=1, keepdims=True)
    lane = lax.broadcasted_iota(jnp.int32, (slots, LANES), 1)
    wide_value = jnp.concatenate(
        [both[:, :frames], jnp.zeros((slots, LANES - frames), jnp.float32)], axis=1
    )
    message[...] = jnp.where(lane == frames, diag, wide_value - removed)


def split3(value):
    a = value.astype(jnp.bfloat16)
    rest = value - a.astype(jnp.float32)
    b = rest.astype(jnp.bfloat16)
    c = (rest - b.astype(jnp.float32)).astype(jnp.bfloat16)
    return a, b, c


def second_exchange(
    frames, message, same, prior, windows, own, new_out, result,
    gathered, grad, grads, send, recv, gsend, grecv,
):
    n = lax.axis_size("bricks")
    me = lax.axis_index("bricks")
    groups = lax.axis_size("frames")
    slots = own.shape[0]
    meet(("bricks", "frames"))
    share_start("bricks", gathered, message, send, recv)
    gathered[me] = message[...]
    share_wait("bricks", gathered, message, send, recv)
    everything = gathered[...].reshape(n * slots, LANES)
    parts = jnp.concatenate(split3(everything), axis=1)
    found = jnp.dot(same[...], parts, preferred_element_type=jnp.float32)
    summed = found[:, :LANES] + found[:, LANES : 2 * LANES] + found[:, 2 * LANES :]
    diag = summed[:, frames : frames + 1]
    new = jnp.maximum(0.0, prior[...] + summed / (diag + 1.0))
    new_out[...] = new[slots:, :frames]
    picked = new[:slots, :frames].astype(jnp.bfloat16)
    gram = lax.dot_general(
        picked, picked, (((1,), (1,)), ((), ())), preferred_element_type=jnp.float32
    )
    g1, g2, g3 = split3(gram)
    none = jnp.zeros((slots, frames), jnp.float32)
    left = jnp.concatenate(
        [
            jnp.concatenate([picked.astype(jnp.float32), -g1.astype(jnp.float32)], axis=1),
            jnp.concatenate([none, -g2.astype(jnp.float32)], axis=1),
            jnp.concatenate([none, -g3.astype(jnp.float32)], axis=1),
        ],
        axis=0,
    ).astype(jnp.bfloat16)
    sub = lax.broadcasted_iota(jnp.int32, (slots, 2 * LANES), 0)
    total = jnp.zeros((slots, 2 * LANES), jnp.float32)
    for k in range(slots):
        one = jnp.dot(left, windows[k], preferred_element_type=jnp.float32)
        one = one[:slots] + one[slots : 2 * slots] + one[2 * slots :]
        total = jnp.where(sub == k, one, total)
    eye = lax.broadcasted_iota(jnp.int32, (slots, slots), 0) == lax.broadcasted_iota(
        jnp.int32, (slots, slots), 1
    )
    gdiag = jnp.sum(jnp.where(eye, gram, 0.0), axis=1, keepdims=True)
    grad[:, : 2 * LANES] = total
    grad[:, 2 * LANES :] = jnp.broadcast_to(gdiag, (slots, LANES))
    share_start("frames", grads, grad, gsend, grecv)
    grads[lax.axis_index("frames")] = grad[...]
    share_wait("frames", grads, grad, gsend, grecv)
    whole = grads[0]
    for g in range(1, groups):
        whole = whole + grads[g]
    current = own[...]
    step = whole[:, : 2 * LANES] / (whole[:, 2 * LANES : 2 * LANES + 1] + 1.0)
    result[...] = jnp.where(current > 0, jnp.maximum(current + step, 0.0), 0.0)


def spread_kernel(tiles, at, result, out):
    slots = out.shape[0]
    first = jnp.broadcast_to(at[...], (slots, LANES))
    second = jnp.where(first + 1 == tiles, 0, first + 1)
    head = result[:, :LANES]
    tail = result[:, LANES:]
    for t in range(tiles):
        out[:, t * LANES : (t + 1) * LANES] = jnp.where(
            first == t, head, jnp.where(second == t, tail, 0.0)
        ).astype(jnp.bfloat16)


def shards(recording, traces, footprints, block_owner, block_slot):
    frames, planes, rows, width = recording.shape
    slots, voxels = footprints.shape
    owned = traces.shape[1]
    n = lax.axis_size("bricks")
    groups = lax.axis_size("frames")
    me = lax.axis_index("bricks")
    tiles = voxels // LANES
    f32 = jnp.float32
    sds = jax.ShapeDtypeStruct
    dma = pltpu.SemaphoreType.DMA
    component = block_owner[:, 0] * owned + block_slot
    rec = jnp.transpose(recording, (1, 2, 0, 3))
    info = jnp.concatenate([traces.T.astype(f32), component.astype(f32)[:, None]], axis=1)

    low, high, infos = pl.pallas_call(
        first_exchange,
        out_shape=(
            sds((SWEEPS, rows, frames, width), jnp.bfloat16),
            sds((SWEEPS, rows, frames, width), jnp.bfloat16),
            sds((n,) + info.shape, f32),
        ),
        in_specs=[VMEM, VMEM],
        out_specs=(VMEM, VMEM, VMEM),
        scratch_shapes=[dma((2,)), dma((2,)), dma((n,)), dma((n,))],
        compiler_params=pltpu.CompilerParams(
            collective_id=0, has_side_effects=True, vmem_limit_bytes=16 << 20
        ),
        name="first_exchange",
    )(rec, info)

    positive = jnp.any((footprints > 0).reshape(slots, tiles, LANES), axis=2)
    begins = positive & ~jnp.roll(positive, 1, axis=1)
    at = jnp.sum(jnp.where(begins, jnp.arange(tiles, dtype=jnp.int32)[None, :], 0), axis=1)

    infos = infos.reshape(n * slots, frames + 1)
    everyone = infos[:, frames].astype(jnp.int32)
    wanted = jnp.concatenate([component, me * owned + jnp.arange(owned, dtype=jnp.int32)])
    same = (wanted[:, None] == everyone[None, :]).astype(jnp.bfloat16)
    picks = (component[:, None] == jnp.arange(n * owned, dtype=jnp.int32)[None, :]).astype(
        jnp.bfloat16
    )
    slot_traces = jnp.dot(
        picks, infos[:, :frames].astype(jnp.bfloat16), preferred_element_type=f32
    )
    prior = jnp.pad(
        jnp.concatenate([slot_traces, traces.T.astype(f32)], axis=0),
        ((0, 0), (0, LANES - frames)),
    )

    message, windows, own = pl.pallas_call(
        functools.partial(local_kernel, tiles),
        out_shape=(
            sds((slots, LANES), f32),
            sds((slots, frames + slots, 2 * LANES), jnp.bfloat16),
            sds((slots, 2 * LANES), f32),
        ),
        in_specs=[SMEM, VMEM, VMEM, VMEM, VMEM, VMEM],
        out_specs=(VMEM, VMEM, VMEM),
        scratch_shapes=[
            pltpu.VMEM((planes + 4, rows, frames, width), f32),
            pltpu.VMEM((planes + 2, rows, frames, width), f32),
            pltpu.VMEM((tiles, frames, LANES), jnp.bfloat16),
            pltpu.VMEM((8, LANES), f32),
        ],
        compiler_params=pltpu.CompilerParams(vmem_limit_bytes=32 << 20),
        name="denoise_project",
    )(at, rec, low, high, footprints, prior[:slots])

    new_t, result = pl.pallas_call(
        functools.partial(second_exchange, frames),
        out_shape=(sds((owned, frames), f32), sds((slots, 2 * LANES), f32)),
        in_specs=[VMEM] * 5,
        out_specs=(VMEM, VMEM),
        scratch_shapes=[
            pltpu.VMEM((n, slots, LANES), f32),
            pltpu.VMEM((slots, 3 * LANES), f32),
            pltpu.VMEM((groups, slots, 3 * LANES), f32),
            dma((n,)),
            dma((n,)),
            dma((groups,)),
            dma((groups,)),
        ],
        compiler_params=pltpu.CompilerParams(
            collective_id=1, has_side_effects=True, vmem_limit_bytes=16 << 20
        ),
        name="second_exchange",
    )(message, same, prior, windows, own)

    footprints_new = pl.pallas_call(
        functools.partial(spread_kernel, tiles),
        out_shape=sds((slots, voxels), jnp.bfloat16),
        in_specs=[VMEM, VMEM],
        out_specs=VMEM,
        name="spread",
    )(at[:, None], result)
    return (new_t.T, footprints_new)


def solution(mesh):
    return jax.shard_map(
        shards,
        mesh=mesh,
        in_specs=(
            P("frames", "bricks", None, None),
            P("frames", "bricks"),
            P("bricks", None),
            P("bricks", None),
            P("bricks"),
        ),
        out_specs=(P("frames", "bricks"), P("bricks", None)),
        check_vma=False,
    )
```

time: 167 us -> 54.5 us (0.33)
  the two profiles are of different devices: /device:TPU:0 before, /device:TPU:10 now
where the time goes in v1:
time: 54.5 us; the launch traced here: 54.2 us
  Pallas kernels  46.4 us (85%)
  local copies, waits for them, and re-layouts  4.65 us (9%)
  other arithmetic  2.27 us (4%)
  between operations  0.72 us (1%)
    pallas_call x1, Pallas kernels, shards(): pl.pallas_call(first_exchange, out_shape=(sds((SWEEPS, rows, frames, widt...  16.5 us
    pallas_call x1, Pallas kernels, shards(): pl.pallas_call(functools.partial(second_exchange, frames), out_shape=(sds...  15.5 us
    pallas_call x1, Pallas kernels, shards(): pl.pallas_call(functools.partial(local_kernel, tiles), out_shape=(sds((sl...  12.2 us
    unnamed x8, local copies, waits for them, and re-layouts  3.02 us
    pallas_call x1, Pallas kernels, shards(): pl.pallas_call(functools.partial(spread_kernel, tiles), out_shape=sds((sl...  2.22 us

profile of v1, /device:TPU:10, one launch (start us, length us, event | category | flops | bytes accessed | tf_op | source)
XLA Modules:
  0.0 54.2 jit_solution(11754721421072819043)
XLA Ops:
  0.6 0.0 copy-start
  0.6 0.8 %convert_bitcast_fusion = (f32[32,1]{0,1:T(1,128)S(1)}, s32[32]{0:T(128)S(1)}, s32[32]{0:T(128)S(1)}) fusion(s32[32]{0:T(128)} %param.9, s32[32,1]{0,1:T(1,128)} %param.8, s32[]{:T(128)S(6)} %mul.15), kind=kLoop, calls=%fused_computation.18 | loop fusion | flops 128 | bytes 644 | tf_op jit(solution)/shard_map/broadcast_in_dim | solution.py:319
  1.4 0.1 pad_add_fusion
  1.5 0.1 copy.37
  1.6 0.8 %copy.36 = f32[16,32]{0,1:T(8,128)S(1)} copy(bf16[16,32]{1,0:T(8,128)(2,1)} %param.6) | data formatting | bytes 3072 | tf_op jit(solution)/shard_map/convert_element_type | solution.py:319
  2.3 0.1 pad_maximum_fusion.info
  2.4 1.3 %copy.47 = bf16[16,4,16,256]{3,0,2,1:T(8,128)(2,1)S(1)} copy(bf16[16,4,16,256]{3,2,1,0:T(8,128)(2,1)} %param.5) | data formatting | bytes 1048576 | tf_op args[0]
  3.8 0.0 copy-done
  3.8 0.3 compare_bitcast_fusion
  4.0 0.3 copy.44
  4.3 0.6 %bitcast_reduce_fusion = pred[32,128]{1,0:T(8,128)(4,1)S(1)} fusion(pred[4,8,128,128]{3,2,1,0:T(8,128)(4,1)S(1)} %copy.44), kind=kLoop, calls=%fused_computation | loop fusion | flops 520192 | bytes 528384 | tf_op jit(solution)/shard_map/reduce_or | solution.py:337
  5.0 0.1 slice.23
  5.1 0.2 select_reduce_fusion.at
  5.2 0.7 %copy.40.at = s32[32,1]{1,0:T(8,128)} copy(s32[32,1]{0,1:T(1,128)S(1)} %bitcast.23) | data formatting | bytes 256 | tf_op jit(solution)/shard_map/broadcast_in_dim | solution.py:401
  5.9 16.5 %first_exchange.1 = (bf16[3,16,16,256]{3,2,1,0:T(8,128)(2,1)S(1)}, bf16[3,16,16,256]{3,2,1,0:T(8,128)(2,1)S(1)}, f32[16,32,17]{2,1,0:T(8,128)S(1)}) custom-call(bf16[4,16,16,256]{3,2,1,0:T(8,128)(2,1)S(1)} %bitcast.18, f32[32,17]{1,0:T(8,128)S(1)} %pad_maximum_fusion.info), custom_call_target="tpu_custom_call" | custom-call | tf_op jit(solution)/shard_map/first_exchange/pallas_call | solution.py:321
  22.5 0.2 fusion
  22.7 0.1 slice_convert_fusion
  22.8 0.1 copy.45
  22.9 12.2 %denoise_project.1 = (f32[32,128]{1,0:T(8,128)S(1)}, bf16[32,48,256]{2,1,0:T(8,128)(2,1)S(1)}, f32[32,256]{1,0:T(8,128)S(1)}) custom-call(s32[32]{0:T(128)S(1)} %select_reduce_fusion.at, bf16[4,16,16,256]{3,2,1,0:T(8,128)(2,1)S(1)} %bitcast.19, bf16[3,16,16,256]{3,2,1,0:T(8,128)(2,1)S(1)} %get-tuple-element.10.low, ...), custom_call_target="tpu_custom_call" | custom-call | tf_op jit(solution)/shard_map/denoise_project/pallas_call | solution.py:356
  35.1 0.1 compare_convert_fusion.same
  35.2 15.5 %second_exchange.1 = (f32[32,16]{1,0:T(8,128)S(1)}, f32[32,256]{1,0:T(8,128)S(1)}) custom-call(f32[32,128]{1,0:T(8,128)S(1)} %get-tuple-element.13.message, bf16[64,512]{1,0:T(8,128)(2,1)S(1)} %compare_convert_fusion.same, f32[64,128]{1,0:T(8,128)S(1)} %select_maximum_fusion.prior, bf16[32,48,256]{2,1,0:T(8,128)(2,1)S(1)} %get-tuple-element.14.windows, ...), custom_call_target="tpu_custom_call" | custom-call | tf_op jit(solution)/shard_map/second_exchange/pallas_call | solution.py:375
  50.7 0.0 copy-start.1
  50.7 0.6 %copy-done.1 = f32[32,256]{1,0:T(8,128)} copy-done((f32[32,256]{1,0:T(8,128)}, f32[32,256]{1,0:T(8,128)S(1)}, u32[]{:S(2)}) %copy-start.1) | copy-done | bytes 32792
  51.3 0.7 %copy.41 = f32[16,32]{1,0:T(8,128)} copy(f32[16,32]{0,1:T(8,128)S(1)} %bitcast.22) | data formatting | bytes 4096
  52.0 2.2 %spread.1 = bf16[32,16384]{1,0:T(8,128)(2,1)} custom-call(s32[32,1]{1,0:T(8,128)} %copy.40.at, f32[32,256]{1,0:T(8,128)} %copy-done.1), custom_call_target="tpu_custom_call" | custom-call | tf_op jit(solution)/shard_map/spread/pallas_call | solution.py:395
  (2 shorter events, 0.0 us)
Async XLA Ops:
  0.6 3.1 %copy-start = (bf16[32,16384]{1,0:T(8,128)(2,1)S(1)}, bf16[32,16384]{1,0:T(8,128)(2,1)}, u32[]{:S(2)}) copy-start(bf16[32,16384]{1,0:T(8,128)(2,1)} %foot.1) | copy-start | bytes 3145732
  50.7 0.6 %copy-start.1 = (f32[32,256]{1,0:T(8,128)}, f32[32,256]{1,0:T(8,128)S(1)}, u32[]{:S(2)}) copy-start(f32[32,256]{1,0:T(8,128)S(1)} %get-tuple-element.17.result) | copy-start | bytes 98308

commit v2 on v1

--- a/solution.py
+++ b/solution.py
@@ -153,8 +153,19 @@
     lax.fori_loop(0, rows, row, first)
 
 
+def side_by_side(ref):
+    return jnp.concatenate([ref[s] for s in range(ref.shape[0])], axis=1)
+
+
+def unpacked(packed, frames, groups):
+    count = frames // groups
+    width = packed.shape[1] // groups
+    cuts = [packed[:count, g * width : (g + 1) * width] for g in range(groups)]
+    return jnp.concatenate(cuts, axis=0), packed[count : count + 1, :width]
+
+
 def local_kernel(
-    tiles, at, rec, low, high, foot, slot_traces, message, windows, own, one, two, y_tiles, zero
+    tiles, at, rec, low, high, foot, infos, picks, message, windows, own, slot_traces, one, two, y_tiles
 ):
     n = lax.axis_size("bricks")
     me = lax.axis_index("bricks")
@@ -192,7 +203,7 @@
     sub = lax.broadcasted_iota(jnp.int32, (slots, 2 * LANES), 0)
     mine = jnp.zeros((slots, 2 * LANES), jnp.float32)
     for k in range(slots):
-        t = at[k]
+        t = at[k, 0]
         u = lax.rem(t + 1, tiles)
         rows_a = jnp.concatenate(
             [
@@ -207,24 +218,30 @@
     own[...] = mine
     mine_bf = mine.astype(jnp.bfloat16)
     wide = frames + slots
-    sub = lax.broadcasted_iota(jnp.int32, (slots, wide), 0)
-    both = jnp.zeros((slots, wide), jnp.float32)
+    lane = lax.broadcasted_iota(jnp.int32, (wide, slots), 1)
+    both = jnp.zeros((wide, slots), jnp.float32)
     for k in range(slots):
         found = lax.dot_general(
-            mine_bf, windows[k], (((1,), (1,)), ((), ())), preferred_element_type=jnp.float32
+            windows[k], mine_bf, (((1,), (1,)), ((), ())), preferred_element_type=jnp.float32
         )
-        both = jnp.where(sub == k, found, both)
-    correlation = both[:, frames:]
-    removed = jnp.dot(correlation, slot_traces[...], precision=HIGHEST)
+        both = jnp.where(lane == k, found, both)
+    correlation = both[frames:]
+    groups = LANES // slots
+    count = frames // groups
+    prior = jnp.dot(
+        side_by_side(infos).astype(jnp.bfloat16), picks[...], preferred_element_type=jnp.float32
+    )
+    prior, _ = unpacked(prior, frames, groups)
+    slot_traces[...] = prior
+    partial = both[:frames] - jnp.dot(prior, correlation, precision=HIGHEST)
     eye = lax.broadcasted_iota(jnp.int32, (slots, slots), 0) == lax.broadcasted_iota(
         jnp.int32, (slots, slots), 1
     )
-    diag = jnp.sum(jnp.where(eye, correlation, 0.0), axis=1, keepdims=True)
-    lane = lax.broadcasted_iota(jnp.int32, (slots, LANES), 1)
-    wide_value = jnp.concatenate(
-        [both[:, :frames], jnp.zeros((slots, LANES - frames), jnp.float32)], axis=1
-    )
-    message[...] = jnp.where(lane == frames, diag, wide_value - removed)
+    diag = jnp.sum(jnp.where(eye, correlation, 0.0), axis=0, keepdims=True)
+    message[...] = jnp.zeros_like(message)
+    for g in range(groups):
+        message[:count, g * slots : (g + 1) * slots] = partial[g * count : (g + 1) * count]
+    message[count : count + 1, :slots] = diag
 
 
 def split3(value):
@@ -247,14 +264,23 @@
     share_start("bricks", gathered, message, send, recv)
     gathered[me] = message[...]
     share_wait("bricks", gathered, message, send, recv)
-    everything = gathered[...].reshape(n * slots, LANES)
-    parts = jnp.concatenate(split3(everything), axis=1)
-    found = jnp.dot(same[...], parts, preferred_element_type=jnp.float32)
-    summed = found[:, :LANES] + found[:, LANES : 2 * LANES] + found[:, 2 * LANES :]
-    diag = summed[:, frames : frames + 1]
+    parts = [part.astype(jnp.float32) for part in split3(side_by_side(gathered))]
+    parts = jnp.concatenate(parts, axis=0).astype(jnp.bfloat16)
+    found = jnp.dot(parts, same[...], preferred_element_type=jnp.float32)
+    high = message.shape[0]
+    found = found[:high] + found[high : 2 * high] + found[2 * high :]
+    summed, diag = unpacked(found, frames, LANES // slots)
     new = jnp.maximum(0.0, prior[...] + summed / (diag + 1.0))
-    new_out[...] = new[slots:, :frames]
-    picked = new[:slots, :frames].astype(jnp.bfloat16)
+    new_out[...] = new[:, slots:]
+    turn = lax.broadcasted_iota(jnp.int32, (slots, slots), 0) == lax.broadcasted_iota(
+        jnp.int32, (slots, slots), 1
+    )
+    picked = lax.dot_general(
+        jnp.where(turn, 1.0, 0.0).astype(jnp.bfloat16),
+        new[:, :slots].astype(jnp.bfloat16),
+        (((1,), (1,)), ((), ())),
+        preferred_element_type=jnp.float32,
+    ).astype(jnp.bfloat16)
     gram = lax.dot_general(
         picked, picked, (((1,), (1,)), ((), ())), preferred_element_type=jnp.float32
     )
@@ -291,16 +317,33 @@
     result[...] = jnp.where(current > 0, jnp.maximum(current + step, 0.0), 0.0)
 
 
-def spread_kernel(tiles, at, result, out):
-    slots = out.shape[0]
-    first = jnp.broadcast_to(at[...], (slots, LANES))
-    second = jnp.where(first + 1 == tiles, 0, first + 1)
+def find_kernel(tiles, foot, at):
+    where = jnp.zeros((foot.shape[0], LANES), jnp.int32)
+    for t in range(tiles):
+        cut = foot[:, t * LANES : (t + 1) * LANES].astype(jnp.float32)
+        where = jnp.where(cut > 0, t, where)
+    at[...] = jnp.broadcast_to(where[:, LANES - 1 :], where.shape)
+
+
+def spread_kernel(tiles, at, result, new, out, new_out):
+    slots, width = out.shape
+    base = pl.program_id(0) * (width // LANES)
+    first = at[...] - base
+    second = jnp.where(at[...] + 1 == tiles, 0, at[...] + 1) - base
     head = result[:, :LANES]
     tail = result[:, LANES:]
-    for t in range(tiles):
+    for t in range(width // LANES):
         out[:, t * LANES : (t + 1) * LANES] = jnp.where(
             first == t, head, jnp.where(second == t, tail, 0.0)
         ).astype(jnp.bfloat16)
+    new_out[...] = new[...]
+
+
+def spread_groups(matches, groups):
+    n, k, m = matches.shape
+    eye = jnp.arange(groups)[:, None] == jnp.arange(groups)[None, :]
+    out = matches[:, None, :, None, :] & eye[None, :, None, :, None]
+    return out.reshape(n * groups * k, groups * m).astype(jnp.bfloat16)
 
 
 def shards(recording, traces, footprints, block_owner, block_slot):
@@ -316,7 +359,21 @@
     dma = pltpu.SemaphoreType.DMA
     component = block_owner[:, 0] * owned + block_slot
     rec = jnp.transpose(recording, (1, 2, 0, 3))
-    info = jnp.concatenate([traces.T.astype(f32), component.astype(f32)[:, None]], axis=1)
+    packs = LANES // slots
+    count = frames // packs
+    high_rows = -(-(count + 1) // 8) * 8
+    info = traces.astype(f32).reshape(packs, count, owned).transpose(1, 0, 2).reshape(count, LANES)
+    extra = jnp.pad(component.astype(f32)[None, :], ((0, high_rows - count - 1), (0, LANES - slots)))
+    info = jnp.concatenate([info, extra], axis=0)
+    at = pl.pallas_call(
+        functools.partial(find_kernel, tiles),
+        out_shape=sds((slots, LANES), jnp.int32),
+        in_specs=[VMEM],
+        out_specs=VMEM,
+        name="find",
+    )(footprints)
+    places = jnp.arange(n * owned, dtype=jnp.int32).reshape(n, owned)
+    picks = spread_groups(places[:, :, None] == component[None, None, :], packs)
 
     low, high, infos = pl.pallas_call(
         first_exchange,
@@ -334,51 +391,37 @@
         name="first_exchange",
     )(rec, info)
 
-    positive = jnp.any((footprints > 0).reshape(slots, tiles, LANES), axis=2)
-    begins = positive & ~jnp.roll(positive, 1, axis=1)
-    at = jnp.sum(jnp.where(begins, jnp.arange(tiles, dtype=jnp.int32)[None, :], 0), axis=1)
-
-    infos = infos.reshape(n * slots, frames + 1)
-    everyone = infos[:, frames].astype(jnp.int32)
-    wanted = jnp.concatenate([component, me * owned + jnp.arange(owned, dtype=jnp.int32)])
-    same = (wanted[:, None] == everyone[None, :]).astype(jnp.bfloat16)
-    picks = (component[:, None] == jnp.arange(n * owned, dtype=jnp.int32)[None, :]).astype(
-        jnp.bfloat16
-    )
-    slot_traces = jnp.dot(
-        picks, infos[:, :frames].astype(jnp.bfloat16), preferred_element_type=f32
-    )
-    prior = jnp.pad(
-        jnp.concatenate([slot_traces, traces.T.astype(f32)], axis=0),
-        ((0, 0), (0, LANES - frames)),
-    )
-
-    message, windows, own = pl.pallas_call(
+    message, windows, own, slot_traces = pl.pallas_call(
         functools.partial(local_kernel, tiles),
         out_shape=(
-            sds((slots, LANES), f32),
+            sds((high_rows, LANES), f32),
             sds((slots, frames + slots, 2 * LANES), jnp.bfloat16),
             sds((slots, 2 * LANES), f32),
-        ),
-        in_specs=[SMEM, VMEM, VMEM, VMEM, VMEM, VMEM],
-        out_specs=(VMEM, VMEM, VMEM),
+            sds((frames, slots), f32),
+        ),
+        in_specs=[SMEM] + [VMEM] * 6,
+        out_specs=(VMEM,) * 4,
         scratch_shapes=[
             pltpu.VMEM((planes + 4, rows, frames, width), f32),
             pltpu.VMEM((planes + 2, rows, frames, width), f32),
             pltpu.VMEM((tiles, frames, LANES), jnp.bfloat16),
-            pltpu.VMEM((8, LANES), f32),
         ],
         compiler_params=pltpu.CompilerParams(vmem_limit_bytes=32 << 20),
         name="denoise_project",
-    )(at, rec, low, high, footprints, prior[:slots])
-
-    new_t, result = pl.pallas_call(
+    )(at, rec, low, high, footprints, infos, picks)
+
+    everyone = infos[:, count, :slots].astype(jnp.int32)
+    wanted = jnp.concatenate([component, me * owned + jnp.arange(owned, dtype=jnp.int32)])
+    same = spread_groups(everyone[:, :, None] == wanted[None, None, :], packs)
+    prior = jnp.concatenate([slot_traces, traces.astype(f32)], axis=1)
+
+    new, result = pl.pallas_call(
         functools.partial(second_exchange, frames),
-        out_shape=(sds((owned, frames), f32), sds((slots, 2 * LANES), f32)),
+        out_shape=(sds((frames, owned), f32), sds((slots, 2 * LANES), f32)),
         in_specs=[VMEM] * 5,
         out_specs=(VMEM, VMEM),
         scratch_shapes=[
-            pltpu.VMEM((n, slots, LANES), f32),
+            pltpu.VMEM((n, high_rows, LANES), f32),
             pltpu.VMEM((slots, 3 * LANES), f32),
             pltpu.VMEM((groups, slots, 3 * LANES), f32),
             dma((n,)),
@@ -392,14 +435,23 @@
         name="second_exchange",
     )(message, same, prior, windows, own)
 
-    footprints_new = pl.pallas_call(
+    steps = 4 if tiles % 4 == 0 else 1
+    footprints_new, traces_new = pl.pallas_call(
         functools.partial(spread_kernel, tiles),
-        out_shape=sds((slots, voxels), jnp.bfloat16),
-        in_specs=[VMEM, VMEM],
-        out_specs=VMEM,
+        out_shape=(sds((slots, voxels), jnp.bfloat16), sds((frames, owned), f32)),
+        grid=(steps,),
+        in_specs=[
+            pl.BlockSpec((slots, LANES), lambda i: (0, 0)),
+            pl.BlockSpec((slots, 2 * LANES), lambda i: (0, 0)),
+            pl.BlockSpec((frames, owned), lambda i: (0, 0)),
+        ],
+        out_specs=(
+            pl.BlockSpec((slots, voxels // steps), lambda i: (0, i)),
+            pl.BlockSpec((frames, owned), lambda i: (0, 0)),
+        ),
         name="spread",
-    )(at[:, None], result)
-    return (new_t.T, footprints_new)
+    )(at, result, new)
+    return (traces_new, footprints_new)
 
 
 def solution(mesh):

time: 54.5 us -> 66.5 us (1.22)
  the two profiles are of different devices: /device:TPU:10 before, /device:TPU:0 now
where the time goes in v2:
time: 66.5 us; the launch traced here: 66 us
  Pallas kernels  46.3 us (70%)
  local copies, waits for them, and re-layouts  11.7 us (18%)
  other arithmetic  7.18 us (11%)
  between operations  0.72 us (1%)
    pallas_call x1, Pallas kernels, shards(): pl.pallas_call(functools.partial(second_exchange, frames), out_shape=(sds...  15.7 us
    pallas_call x1, Pallas kernels, shards(): pl.pallas_call(first_exchange, out_shape=(sds((SWEEPS, rows, frames, widt...  13.5 us
    pallas_call x1, Pallas kernels, shards(): pl.pallas_call(functools.partial(local_kernel, tiles), out_shape=(sds((hi...  12.6 us
    convert_element_type x2, local copies, waits for them, and re-layouts, spread_groups(): return out.reshape(n * groups * k, groups * m).astype(jnp.bfloat16)  6.63 us
    convert_element_type x2, other arithmetic, spread_groups(): return out.reshape(n * groups * k, groups * m).astype(jnp.bfloat16)  5.34 us
    unnamed x13, local copies, waits for them, and re-layouts  4.99 us
    pallas_call x1, Pallas kernels, shards(): pl.pallas_call(functools.partial(spread_kernel, tiles), out_shape=(sds((s...  2.45 us
    pallas_call x1, Pallas kernels, shards(): pl.pallas_call(functools.partial(find_kernel, tiles), out_shape=sds((slot...  2.12 us

profile of v2, /device:TPU:0, one launch (start us, length us, event | category | flops | bytes accessed | tf_op | source)
XLA Modules:
  0.0 66.0 jit_solution(4846694252668838643)
XLA Ops:
  0.6 0.7 %convert_bitcast_fusion = (f32[1,32]{1,0:T(1,128)S(1)}, s32[32]{0:T(128)S(1)}, s32[32]{0:T(128)S(1)}) fusion(s32[32]{0:T(128)} %param.9, s32[32,1]{0,1:T(1,128)} %param.8, s32[]{:T(128)S(6)} %mul.15), kind=kLoop, calls=%fused_computation.14 | loop fusion | flops 128 | bytes 644 | tf_op jit(solution)/shard_map/broadcast_in_dim | solution.py:366
  1.3 0.7 %convert_element_type.29 = f32[16,32]{1,0:T(8,128)S(1)} convert(bf16[16,32]{1,0:T(8,128)(2,1)} %param.6) | non-fusion elementwise | flops 512 | bytes 3072 | tf_op jit(solution)/shard_map/convert_element_type | solution.py:365
  2.0 0.1 reshape.58
  2.1 1.3 %copy.10 = bf16[16,4,16,256]{3,0,2,1:T(8,128)(2,1)S(1)} copy(bf16[16,4,16,256]{3,2,1,0:T(8,128)(2,1)} %param.5) | data formatting | bytes 1048576 | tf_op args[0]
  3.4 13.5 %first_exchange.1 = (bf16[3,16,16,256]{3,2,1,0:T(8,128)(2,1)S(1)}, bf16[3,16,16,256]{3,2,1,0:T(8,128)(2,1)S(1)}, f32[16,8,128]{2,1,0:T(8,128)S(1)}) custom-call(bf16[4,16,16,256]{3,2,1,0:T(8,128)(2,1)S(1)} %bitcast.12, f32[8,128]{1,0:T(8,128)S(1)} %select_maximum_fusion.info), custom_call_target="tpu_custom_call" | custom-call | tf_op jit(solution)/shard_map/first_exchange/pallas_call | solution.py:378
  16.9 0.0 copy-start.1
  16.9 0.7 %copy-done.1 = bf16[3,16,16,256]{3,2,1,0:T(8,128)(2,1)} copy-done((bf16[3,16,16,256]{3,2,1,0:T(8,128)(2,1)}, bf16[3,16,16,256]{3,2,1,0:T(8,128)(2,1)S(1)}, u32[]{:S(2)}) %copy-start.1) | copy-done | bytes 393240
  17.7 0.1 broadcast_compare_fusion.1
  17.8 2.7 %and_convert_fusion.1 = bf16[16,4,32,4,32]{4,3,2,1,0:T(4,128)(2,1)} fusion(pred[4,4]{1,0:T(4,128)(4,1)S(1)} %iota_compare_fusion.1, pred[16,32,32]{2,1,0:T(8,128)(4,1)S(1)} %broadcast_compare_fusion.1), kind=kLoop, calls=%fused_computation.1 | loop fusion | flops 524288 | bytes 540688 | tf_op jit(solution)/shard_map/convert_element_type | solution.py:346
  20.5 0.0 copy-start
  20.5 3.2 %reshape.59.picks = bf16[2048,128]{1,0:T(8,128)(2,1)S(1)} reshape(bf16[16,4,32,4,32]{4,3,2,1,0:T(4,128)(2,1)} %and_convert_fusion.1) | data formatting | bytes 1048576 | tf_op jit(solution)/shard_map/convert_element_type | solution.py:346
  23.7 2.1 %find.1.at = s32[32,128]{1,0:T(8,128)} custom-call(bf16[32,16384]{1,0:T(8,128)(2,1)} %foot.3), custom_call_target="tpu_custom_call" | custom-call | tf_op jit(solution)/shard_map/find/pallas_call | solution.py:368
  25.8 0.0 copy-done
  25.8 0.0 copy-start.2
  25.8 1.0 %copy-done.2 = bf16[3,16,16,256]{3,2,1,0:T(8,128)(2,1)S(1)} copy-done((bf16[3,16,16,256]{3,2,1,0:T(8,128)(2,1)S(1)}, bf16[3,16,16,256]{3,2,1,0:T(8,128)(2,1)}, u32[]{:S(2)}) %copy-start.2) | copy-done | bytes 393240
  26.8 0.0 copy-start.3
  26.8 0.7 %copy-done.3 = s32[32,128]{1,0:T(8,128)S(1)} copy-done((s32[32,128]{1,0:T(8,128)S(1)}, s32[32,128]{1,0:T(8,128)}, u32[]{:S(2)}) %copy-start.3) | copy-done | bytes 16408
  27.5 12.6 %denoise_project.1 = (f32[8,128]{1,0:T(8,128)S(1)}, bf16[32,48,256]{2,1,0:T(8,128)(2,1)S(1)}, f32[32,256]{1,0:T(8,128)S(1)}, f32[16,32]{1,0:T(8,128)S(1)}) custom-call(s32[32,128]{1,0:T(8,128)S(1)} %copy-done.3, bf16[4,16,16,256]{3,2,1,0:T(8,128)(2,1)S(1)} %bitcast.13, bf16[3,16,16,256]{3,2,1,0:T(8,128)(2,1)S(1)} %get-tuple-element.13.low, ...), custom_call_target="tpu_custom_call" | custom-call | tf_op jit(solution)/shard_map/denoise_project/pallas_call | solution.py:394
  40.1 0.1 pad_maximum_fusion.prior
  40.2 0.1 pad_add_fusion
  40.3 0.1 broadcast_compare_fusion
  40.5 2.7 %and_convert_fusion = bf16[16,4,32,4,64]{4,3,2,1,0:T(4,128)(2,1)} fusion(pred[4,4]{1,0:T(4,128)(4,1)S(1)} %iota_compare_fusion.1, pred[16,32,64]{2,1,0:T(8,128)(4,1)S(1)} %broadcast_compare_fusion), kind=kLoop, calls=%fused_computation | loop fusion | flops 1048576 | bytes 1081360 | tf_op jit(solution)/shard_map/convert_element_type | solution.py:346
  43.1 3.5 %reshape.60.same = bf16[2048,256]{1,0:T(8,128)(2,1)S(1)} reshape(bf16[16,4,32,4,64]{4,3,2,1,0:T(4,128)(2,1)} %and_convert_fusion) | data formatting | bytes 2097152 | tf_op jit(solution)/shard_map/convert_element_type | solution.py:346
  46.6 15.7 %second_exchange.1 = (f32[16,32]{1,0:T(8,128)S(1)}, f32[32,256]{1,0:T(8,128)S(1)}) custom-call(f32[8,128]{1,0:T(8,128)S(1)} %get-tuple-element.16.message, bf16[2048,256]{1,0:T(8,128)(2,1)S(1)} %reshape.60.same, f32[16,64]{1,0:T(8,128)S(1)} %pad_maximum_fusion.prior, bf16[32,48,256]{2,1,0:T(8,128)(2,1)S(1)} %get-tuple-element.18.windows, ...), custom_call_target="tpu_custom_call" | custom-call | tf_op jit(solution)/shard_map/second_exchange/pallas_call | solution.py:418
  62.3 0.0 copy-start.4
  62.3 0.6 copy-done.4
  62.9 0.0 copy-start.5
  62.9 0.6 copy-done.5
  63.5 2.5 %spread.1 = (bf16[32,16384]{1,0:T(8,128)(2,1)}, f32[16,32]{1,0:T(8,128)}) custom-call(s32[32,128]{1,0:T(8,128)} %find.1.at, f32[32,256]{1,0:T(8,128)} %copy-done.4, f32[16,32]{1,0:T(8,128)} %copy-done.5), custom_call_target="tpu_custom_call" | custom-call | tf_op jit(solution)/shard_map/spread/pallas_call | solution.py:439
  (5 shorter events, 0.0 us)
Async XLA Ops:
  16.9 0.7 %copy-start.1 = (bf16[3,16,16,256]{3,2,1,0:T(8,128)(2,1)}, bf16[3,16,16,256]{3,2,1,0:T(8,128)(2,1)S(1)}, u32[]{:S(2)}) copy-start(bf16[3,16,16,256]{3,2,1,0:T(8,128)(2,1)S(1)} %get-tuple-element.14.high) | copy-start | bytes 1179652
  20.5 5.3 %copy-start = (bf16[32,16384]{1,0:T(8,128)(2,1)S(1)}, bf16[32,16384]{1,0:T(8,128)(2,1)}, u32[]{:S(2)}) copy-start(bf16[32,16384]{1,0:T(8,128)(2,1)} %foot.3) | copy-start | bytes 3145732
  25.8 1.0 %copy-start.2 = (bf16[3,16,16,256]{3,2,1,0:T(8,128)(2,1)S(1)}, bf16[3,16,16,256]{3,2,1,0:T(8,128)(2,1)}, u32[]{:S(2)}) copy-start(bf16[3,16,16,256]{3,2,1,0:T(8,128)(2,1)} %copy-done.1) | copy-start | bytes 1179652
  26.8 0.7 %copy-start.3 = (s32[32,128]{1,0:T(8,128)S(1)}, s32[32,128]{1,0:T(8,128)}, u32[]{:S(2)}) copy-start(s32[32,128]{1,0:T(8,128)} %find.1.at) | copy-start | bytes 49156
  62.3 0.6 copy-start.4
  62.9 0.6 copy-start.5

commit v3 on v2

--- a/solution.py
+++ b/solution.py
@@ -63,7 +63,16 @@
     lax.fori_loop(1, lax.axis_size(axis), go, 0)
 
 
-def first_exchange(rec, info, low, high, infos, hsend, hrecv, send, recv):
+def find_first(foot, at):
+    tiles = foot.shape[1] // LANES
+    where = jnp.zeros((foot.shape[0], LANES), jnp.int32)
+    for t in range(tiles):
+        cut = foot[:, t * LANES : (t + 1) * LANES].astype(jnp.float32)
+        where = jnp.where(cut > 0, t, where)
+    at[...] = jnp.broadcast_to(where[:, LANES - 1 :], where.shape)
+
+
+def first_exchange(rec, info, foot, low, high, infos, at, hsend, hrecv, send, recv):
     n = lax.axis_size("bricks")
     me = lax.axis_index("bricks")
     planes = rec.shape[0]
@@ -95,6 +104,7 @@
 
     share_start("bricks", infos, info, send, recv)
     infos[me] = info[...]
+    find_first(foot, at)
 
     @pl.when(me == 0)
     def _():
@@ -165,7 +175,7 @@
 
 
 def local_kernel(
-    tiles, at, rec, low, high, foot, infos, picks, message, windows, own, slot_traces, one, two, y_tiles
+    tiles, at, rec, low, high, foot, infos, columns, message, windows, own, slot_traces, one, two, y_tiles
 ):
     n = lax.axis_size("bricks")
     me = lax.axis_index("bricks")
@@ -228,8 +238,14 @@
     correlation = both[frames:]
     groups = LANES // slots
     count = frames // groups
-    prior = jnp.dot(
-        side_by_side(infos).astype(jnp.bfloat16), picks[...], preferred_element_type=jnp.float32
+    lane = lax.broadcasted_iota(jnp.int32, (LANES, n * LANES), 1)
+    place = (lane // LANES * slots + lane % slots) * groups + lane % LANES // slots
+    picks = jnp.where(place == columns[...], 1.0, 0.0).astype(jnp.bfloat16)
+    prior = lax.dot_general(
+        side_by_side(infos).astype(jnp.bfloat16),
+        picks,
+        (((1,), (1,)), ((), ())),
+        preferred_element_type=jnp.float32,
     )
     prior, _ = unpacked(prior, frames, groups)
     slot_traces[...] = prior
@@ -253,8 +269,8 @@
 
 
 def second_exchange(
-    frames, message, same, prior, windows, own, new_out, result,
-    gathered, grad, grads, send, recv, gsend, grecv,
+    frames, message, infos, wanted, prior, windows, own, new_out, result,
+    gathered, same, grad, grads, send, recv, gsend, grecv,
 ):
     n = lax.axis_size("bricks")
     me = lax.axis_index("bricks")
@@ -263,10 +279,18 @@
     meet(("bricks", "frames"))
     share_start("bricks", gathered, message, send, recv)
     gathered[me] = message[...]
+    count = frames // (LANES // slots)
+    for s in range(n):
+        row = infos[s][count : count + 1, :]
+        same[:, s * LANES : (s + 1) * LANES] = jnp.where(wanted[...] == row, 1.0, 0.0).astype(
+            jnp.bfloat16
+        )
     share_wait("bricks", gathered, message, send, recv)
     parts = [part.astype(jnp.float32) for part in split3(side_by_side(gathered))]
     parts = jnp.concatenate(parts, axis=0).astype(jnp.bfloat16)
-    found = jnp.dot(parts, same[...], preferred_element_type=jnp.float32)
+    found = lax.dot_general(
+        parts, same[...], (((1,), (1,)), ((), ())), preferred_element_type=jnp.float32
+    )
     high = message.shape[0]
     found = found[:high] + found[high : 2 * high] + found[2 * high :]
     summed, diag = unpacked(found, frames, LANES // slots)
@@ -317,14 +341,6 @@
     result[...] = jnp.where(current > 0, jnp.maximum(current + step, 0.0), 0.0)
 
 
-def find_kernel(tiles, foot, at):
-    where = jnp.zeros((foot.shape[0], LANES), jnp.int32)
-    for t in range(tiles):
-        cut = foot[:, t * LANES : (t + 1) * LANES].astype(jnp.float32)
-        where = jnp.where(cut > 0, t, where)
-    at[...] = jnp.broadcast_to(where[:, LANES - 1 :], where.shape)
-
-
 def spread_kernel(tiles, at, result, new, out, new_out):
     slots, width = out.shape
     base = pl.program_id(0) * (width // LANES)
@@ -337,13 +353,6 @@
             first == t, head, jnp.where(second == t, tail, 0.0)
         ).astype(jnp.bfloat16)
     new_out[...] = new[...]
-
-
-def spread_groups(matches, groups):
-    n, k, m = matches.shape
-    eye = jnp.arange(groups)[:, None] == jnp.arange(groups)[None, :]
-    out = matches[:, None, :, None, :] & eye[None, :, None, :, None]
-    return out.reshape(n * groups * k, groups * m).astype(jnp.bfloat16)
 
 
 def shards(recording, traces, footprints, block_owner, block_slot):
@@ -363,33 +372,31 @@
     count = frames // packs
     high_rows = -(-(count + 1) // 8) * 8
     info = traces.astype(f32).reshape(packs, count, owned).transpose(1, 0, 2).reshape(count, LANES)
-    extra = jnp.pad(component.astype(f32)[None, :], ((0, high_rows - count - 1), (0, LANES - slots)))
+    extra = component[None, :] * packs + jnp.arange(packs, dtype=jnp.int32)[:, None]
+    extra = jnp.pad(extra.astype(f32).reshape(1, LANES), ((0, high_rows - count - 1), (0, 0)))
     info = jnp.concatenate([info, extra], axis=0)
-    at = pl.pallas_call(
-        functools.partial(find_kernel, tiles),
-        out_shape=sds((slots, LANES), jnp.int32),
-        in_specs=[VMEM],
-        out_specs=VMEM,
-        name="find",
-    )(footprints)
-    places = jnp.arange(n * owned, dtype=jnp.int32).reshape(n, owned)
-    picks = spread_groups(places[:, :, None] == component[None, None, :], packs)
-
-    low, high, infos = pl.pallas_call(
+    order = jnp.arange(packs, dtype=jnp.int32)[:, None]
+    columns = (component[None, :] * packs + order).reshape(packs * slots, 1)
+    mine = me * owned + jnp.arange(owned, dtype=jnp.int32)
+    both = jnp.concatenate([component, mine])
+    wanted = (both[None, :] * packs + order).reshape(packs * (slots + owned), 1).astype(f32)
+
+    low, high, infos, at = pl.pallas_call(
         first_exchange,
         out_shape=(
             sds((SWEEPS, rows, frames, width), jnp.bfloat16),
             sds((SWEEPS, rows, frames, width), jnp.bfloat16),
             sds((n,) + info.shape, f32),
-        ),
-        in_specs=[VMEM, VMEM],
-        out_specs=(VMEM, VMEM, VMEM),
+            sds((slots, LANES), jnp.int32),
+        ),
+        in_specs=[VMEM] * 3,
+        out_specs=(VMEM,) * 4,
         scratch_shapes=[dma((2,)), dma((2,)), dma((n,)), dma((n,))],
         compiler_params=pltpu.CompilerParams(
             collective_id=0, has_side_effects=True, vmem_limit_bytes=16 << 20
         ),
         name="first_exchange",
-    )(rec, info)
+    )(rec, info, footprints)
 
     message, windows, own, slot_traces = pl.pallas_call(
         functools.partial(local_kernel, tiles),
@@ -408,20 +415,18 @@
         ],
         compiler_params=pltpu.CompilerParams(vmem_limit_bytes=32 << 20),
         name="denoise_project",
-    )(at, rec, low, high, footprints, infos, picks)
-
-    everyone = infos[:, count, :slots].astype(jnp.int32)
-    wanted = jnp.concatenate([component, me * owned + jnp.arange(owned, dtype=jnp.int32)])
-    same = spread_groups(everyone[:, :, None] == wanted[None, None, :], packs)
+    )(at, rec, low, high, footprints, infos, columns)
+
     prior = jnp.concatenate([slot_traces, traces.astype(f32)], axis=1)
 
     new, result = pl.pallas_call(
         functools.partial(second_exchange, frames),
         out_shape=(sds((frames, owned), f32), sds((slots, 2 * LANES), f32)),
-        in_specs=[VMEM] * 5,
+        in_specs=[VMEM] * 6,
         out_specs=(VMEM, VMEM),
         scratch_shapes=[
             pltpu.VMEM((n, high_rows, LANES), f32),
+            pltpu.VMEM((packs * (slots + owned), n * LANES), jnp.bfloat16),
             pltpu.VMEM((slots, 3 * LANES), f32),
             pltpu.VMEM((groups, slots, 3 * LANES), f32),
             dma((n,)),
@@ -433,7 +438,7 @@
             collective_id=1, has_side_effects=True, vmem_limit_bytes=16 << 20
         ),
         name="second_exchange",
-    )(message, same, prior, windows, own)
+    )(message, infos, wanted, prior, windows, own)
 
     steps = 4 if tiles % 4 == 0 else 1
     footprints_new, traces_new = pl.pallas_call(

time: 66.5 us -> 50.7 us (0.76)
  local copies, waits for them, and re-layouts: 11.7 us -> 3.44 us
  other arithmetic: 7.18 us -> 1.66 us
  Pallas kernels: 46.3 us -> 44.7 us
    convert_element_type x2, local copies, waits for them, and re-layouts: 6.63 us -> 0.23 us  [the longest x1 0.15 us: shards(): (both[None, :] * packs + order).reshape(packs * (slots + owned), 1)]
    convert_element_type x3 -> x1, other arithmetic: 5.36 us -> 0.01 us  [shards(): (both[None, :] * packs + order).reshape(packs * (slots + owned), 1)]
    pallas_call x1 -> x0, Pallas kernels: 2.12 us -> none  [shards(): pl.pallas_call(functools.partial(find_kernel, tiles), out_shape=sds((slot...]
    unnamed x13 -> x9, local copies, waits for them, and re-layouts: 4.99 us -> 3.02 us
    mul x0 -> x2, other arithmetic: none -> 0.84 us  [the longest x1 0.77 us: shards(): component[None, :] * packs + jnp.arange(packs, dtype=jnp.int32)[:, None]]
    broadcast_in_dim x1 -> x0, other arithmetic: 0.68 us -> none  [shards(): component.astype(f32)[None, :]]
where the time goes in v3:
time: 50.7 us; the launch traced here: 50.5 us
  Pallas kernels  44.7 us (88%)
  local copies, waits for them, and re-layouts  3.44 us (7%)
  other arithmetic  1.66 us (3%)
  between operations  0.71 us (1%)
    pallas_call x1, Pallas kernels, shards(): pl.pallas_call(functools.partial(second_exchange, frames), out_shape=(sds...  16.1 us
    pallas_call x1, Pallas kernels, shards(): pl.pallas_call(first_exchange, out_shape=(sds((SWEEPS, rows, frames, widt...  13.5 us
    pallas_call x1, Pallas kernels, shards(): pl.pallas_call(functools.partial(local_kernel, tiles), out_shape=(sds((hi...  12.7 us
    unnamed x9, local copies, waits for them, and re-layouts  3.02 us
    pallas_call x1, Pallas kernels, shards(): pl.pallas_call(functools.partial(spread_kernel, tiles), out_shape=(sds((s...  2.45 us

profile of v3, /device:TPU:0, one launch (start us, length us, event | category | flops | bytes accessed | tf_op | source)
XLA Modules:
  0.0 50.5 jit_solution(17307684423276893339)
XLA Ops:
  0.6 0.0 copy-start
  0.6 0.8 %broadcast_multiply_fusion = (s32[32]{0:T(128)S(1)}, s32[32]{0:T(128)S(1)}, s32[32]{0:T(128)S(1)}) fusion(s32[32]{0:T(128)} %param.9, s32[32,1]{0,1:T(1,128)} %param.8, s32[]{:T(128)S(6)} %mul.32), kind=kLoop, calls=%fused_computation.10 | loop fusion | flops 128 | bytes 644 | tf_op jit(solution)/shard_map/mul | solution.py:375
  1.4 0.1 convert_element_type.26
  1.5 0.7 %convert_element_type.24 = f32[16,32]{1,0:T(8,128)S(1)} convert(bf16[16,32]{1,0:T(8,128)(2,1)} %param.6) | non-fusion elementwise | flops 512 | bytes 3072 | tf_op jit(solution)/shard_map/convert_element_type | solution.py:374
  2.2 0.1 reshape.107
  2.3 1.3 %copy.15 = bf16[16,4,16,256]{3,0,2,1:T(8,128)(2,1)S(1)} copy(bf16[16,4,16,256]{3,2,1,0:T(8,128)(2,1)} %param.5) | data formatting | bytes 1048576 | tf_op args[0]
  3.6 0.0 copy-done
  3.6 13.5 %first_exchange.1 = (bf16[3,16,16,256]{3,2,1,0:T(8,128)(2,1)S(1)}, bf16[3,16,16,256]{3,2,1,0:T(8,128)(2,1)S(1)}, f32[16,8,128]{2,1,0:T(8,128)S(1)}, s32[32,128]{1,0:T(8,128)S(1)}) custom-call(bf16[4,16,16,256]{3,2,1,0:T(8,128)(2,1)S(1)} %bitcast.9, f32[8,128]{1,0:T(8,128)S(1)} %select_maximum_fusion.info, bf16[32,16384]{1,0:T(8,128)(2,1)S(1)} %copy-done), custom_call_target="tpu_custom_call" | custom-call | tf_op jit(solution)/shard_map/first_exchange/pallas_call | solution.py:384
  17.1 0.0 copy-start.1
  17.1 0.1 add.83.columns
  17.2 0.5 copy-done.1
  17.7 12.7 %denoise_project.1 = (f32[8,128]{1,0:T(8,128)S(1)}, bf16[32,48,256]{2,1,0:T(8,128)(2,1)S(1)}, f32[32,256]{1,0:T(8,128)S(1)}, f32[16,32]{1,0:T(8,128)S(1)}) custom-call(s32[32,128]{1,0:T(8,128)S(1)} %get-tuple-element.14.at, bf16[4,16,16,256]{3,2,1,0:T(8,128)(2,1)S(1)} %bitcast.10, bf16[3,16,16,256]{3,2,1,0:T(8,128)(2,1)S(1)} %get-tuple-element.15.low, ...), custom_call_target="tpu_custom_call" | custom-call | tf_op jit(solution)/shard_map/denoise_project/pallas_call | solution.py:401
  30.4 0.1 pad_maximum_fusion.prior
  30.5 0.1 add_multiply_fusion
  30.6 0.1 convert_element_type.29.wanted
  30.7 16.1 %second_exchange.1 = (f32[16,32]{1,0:T(8,128)S(1)}, f32[32,256]{1,0:T(8,128)S(1)}) custom-call(f32[8,128]{1,0:T(8,128)S(1)} %get-tuple-element.18.message, f32[16,8,128]{2,1,0:T(8,128)S(1)} %get-tuple-element.17.infos, f32[256,1]{1,0:T(8,128)S(1)} %convert_element_type.29.wanted, f32[16,64]{1,0:T(8,128)S(1)} %pad_maximum_fusion.prior, ...), custom_call_target="tpu_custom_call" | custom-call | tf_op jit(solution)/shard_map/second_exchange/pallas_call | solution.py:422
  46.8 0.0 copy-start.2
  46.8 0.6 %copy-done.2 = f32[32,256]{1,0:T(8,128)} copy-done((f32[32,256]{1,0:T(8,128)}, f32[32,256]{1,0:T(8,128)S(1)}, u32[]{:S(2)}) %copy-start.2) | copy-done | bytes 32792
  47.4 0.0 copy-start.3
  47.4 0.6 %copy-done.3 = f32[16,32]{1,0:T(8,128)} copy-done((f32[16,32]{1,0:T(8,128)}, f32[16,32]{1,0:T(8,128)S(1)}, u32[]{:S(2)}) %copy-start.3) | copy-done | bytes 2072
  48.0 2.5 %spread.1 = (bf16[32,16384]{1,0:T(8,128)(2,1)}, f32[16,32]{1,0:T(8,128)}) custom-call(s32[32,128]{1,0:T(8,128)} %copy-done.1, f32[32,256]{1,0:T(8,128)} %copy-done.2, f32[16,32]{1,0:T(8,128)} %copy-done.3), custom_call_target="tpu_custom_call" | custom-call | tf_op jit(solution)/shard_map/spread/pallas_call | solution.py:444
  (4 shorter events, 0.0 us)
Async XLA Ops:
  0.6 3.0 %copy-start = (bf16[32,16384]{1,0:T(8,128)(2,1)S(1)}, bf16[32,16384]{1,0:T(8,128)(2,1)}, u32[]{:S(2)}) copy-start(bf16[32,16384]{1,0:T(8,128)(2,1)} %foot.3) | copy-start | bytes 3145732
  17.1 0.6 %copy-start.1 = (s32[32,128]{1,0:T(8,128)}, s32[32,128]{1,0:T(8,128)S(1)}, u32[]{:S(2)}) copy-start(s32[32,128]{1,0:T(8,128)S(1)} %get-tuple-element.14.at) | copy-start | bytes 49156
  46.8 0.6 %copy-start.2 = (f32[32,256]{1,0:T(8,128)}, f32[32,256]{1,0:T(8,128)S(1)}, u32[]{:S(2)}) copy-start(f32[32,256]{1,0:T(8,128)S(1)} %get-tuple-element.22.result) | copy-start | bytes 98308
  47.4 0.6 %copy-start.3 = (f32[16,32]{1,0:T(8,128)}, f32[16,32]{1,0:T(8,128)S(1)}, u32[]{:S(2)}) copy-start(f32[16,32]{1,0:T(8,128)S(1)} %get-tuple-element.23.new) | copy-start | bytes 6148

commit v4 on v3

--- a/solution.py
+++ b/solution.py
@@ -9,6 +9,7 @@
 
 TIME_STEP = 0.14
 SWEEPS = 3
+CUTS = 4
 LANES = 128
 HIGHEST = lax.Precision.HIGHEST
 MESH = pl.DeviceIdType.MESH
@@ -72,68 +73,13 @@
     at[...] = jnp.broadcast_to(where[:, LANES - 1 :], where.shape)
 
 
-def first_exchange(rec, info, foot, low, high, infos, at, hsend, hrecv, send, recv):
-    n = lax.axis_size("bricks")
-    me = lax.axis_index("bricks")
-    planes = rec.shape[0]
-    meet(("bricks",))
-    to_right = pltpu.make_async_remote_copy(
-        src_ref=rec.at[pl.ds(planes - SWEEPS, SWEEPS)],
-        dst_ref=low,
-        send_sem=hsend.at[0],
-        recv_sem=hrecv.at[0],
-        device_id={"bricks": lax.rem(me + 1, n)},
-        device_id_type=MESH,
-    )
-    to_left = pltpu.make_async_remote_copy(
-        src_ref=rec.at[pl.ds(0, SWEEPS)],
-        dst_ref=high,
-        send_sem=hsend.at[1],
-        recv_sem=hrecv.at[1],
-        device_id={"bricks": lax.rem(me + n - 1, n)},
-        device_id_type=MESH,
-    )
-
-    @pl.when(me < n - 1)
-    def _():
-        to_right.start()
-
-    @pl.when(me > 0)
-    def _():
-        to_left.start()
-
-    share_start("bricks", infos, info, send, recv)
-    infos[me] = info[...]
-    find_first(foot, at)
-
-    @pl.when(me == 0)
-    def _():
-        low[...] = jnp.zeros_like(low)
-
-    @pl.when(me == n - 1)
-    def _():
-        high[...] = jnp.zeros_like(high)
-
-    share_wait("bricks", infos, info, send, recv)
-
-    @pl.when(me < n - 1)
-    def _():
-        to_right.wait_send()
-        to_left.wait_recv()
-
-    @pl.when(me > 0)
-    def _():
-        to_left.wait_send()
-        to_right.wait_recv()
-
-
 def flux_of(difference):
     below = 1.0 + difference * difference
     near = pl.reciprocal(below, approx=True)
     return difference * (near * (2.0 - below * near))
 
 
-def sweep(load, store, planes, rows, shape):
+def sweep(load, store, planes, rows, shape, low_row, high_row, first):
     lane = lax.broadcasted_iota(jnp.int32, shape, 1)
     width = shape[1]
 
@@ -159,30 +105,59 @@
             center = right
         return tuple(out)
 
-    first = tuple(flux_of(load(x + 1, 0)) for x in range(planes))
-    lax.fori_loop(0, rows, row, first)
-
-
-def side_by_side(ref):
-    return jnp.concatenate([ref[s] for s in range(ref.shape[0])], axis=1)
-
-
-def unpacked(packed, frames, groups):
-    count = frames // groups
-    width = packed.shape[1] // groups
-    cuts = [packed[:count, g * width : (g + 1) * width] for g in range(groups)]
-    return jnp.concatenate(cuts, axis=0), packed[count : count + 1, :width]
-
-
-def local_kernel(
-    tiles, at, rec, low, high, foot, infos, columns, message, windows, own, slot_traces, one, two, y_tiles
+    if first is None:
+        first = tuple(flux_of(load(x + 1, 0)) for x in range(planes))
+    return lax.fori_loop(low_row, high_row, row, first)
+
+
+def first_exchange(
+    rec, info, foot, y_tiles, infos, at, low, high, one, two, hsend, hrecv, send, recv
 ):
     n = lax.axis_size("bricks")
     me = lax.axis_index("bricks")
     planes, rows, frames, width = rec.shape
-    slots = foot.shape[0]
     shape = (frames, width)
     per = width // LANES
+    cuts = CUTS if rows % CUTS == 0 and rows // CUTS > SWEEPS else 1
+    part = rows // cuts
+    meet(("bricks",))
+
+    def copies(c):
+        at_rows = pl.ds(c * part, part)
+        to_right = pltpu.make_async_remote_copy(
+            src_ref=rec.at[pl.ds(planes - SWEEPS, SWEEPS), at_rows],
+            dst_ref=low.at[:, at_rows],
+            send_sem=hsend.at[0, c],
+            recv_sem=hrecv.at[0, c],
+            device_id={"bricks": lax.rem(me + 1, n)},
+            device_id_type=MESH,
+        )
+        to_left = pltpu.make_async_remote_copy(
+            src_ref=rec.at[pl.ds(0, SWEEPS), at_rows],
+            dst_ref=high.at[:, at_rows],
+            send_sem=hsend.at[1, c],
+            recv_sem=hrecv.at[1, c],
+            device_id={"bricks": lax.rem(me + n - 1, n)},
+            device_id_type=MESH,
+        )
+        return to_right, to_left
+
+    for c in range(cuts):
+        to_right, to_left = copies(c)
+        pl.when(me < n - 1)(to_right.start)
+        pl.when(me > 0)(to_left.start)
+    share_start("bricks", infos, info, send, recv)
+    infos[me] = info[...]
+
+    @pl.when(me == 0)
+    def _():
+        low[...] = jnp.zeros_like(low)
+
+    @pl.when(me == n - 1)
+    def _():
+        high[...] = jnp.zeros_like(high)
+
+    find_first(foot, at)
 
     def load_first(x, z):
         if x < SWEEPS:
@@ -206,10 +181,44 @@
         for h in range(per):
             y_tiles[(x * rows + z) * per + h] = value[:, h * LANES : (h + 1) * LANES]
 
-    sweep(load_first, keep(one, 2), planes + 4, rows, shape)
-    sweep(lambda x, z: one[x, z], keep(two, 1), planes + 2, rows, shape)
-    sweep(lambda x, z: two[x, z], store_last, planes, rows, shape)
-
+    loads = (load_first, lambda x, z: one[x, z], lambda x, z: two[x, z])
+    stores = (keep(one, 2), keep(two, 1), store_last)
+    carried = [None] * SWEEPS
+    done = [0] * SWEEPS
+    for c in range(cuts):
+        to_right, to_left = copies(c)
+        pl.when(me > 0)(to_right.wait_recv)
+        pl.when(me < n - 1)(to_left.wait_recv)
+        for i in range(SWEEPS):
+            end = rows if c == cuts - 1 else (c + 1) * part - 1 - i
+            carried[i] = sweep(
+                loads[i], stores[i], planes + 2 * (SWEEPS - 1 - i), rows, shape, done[i], end, carried[i]
+            )
+            done[i] = end
+    for c in range(cuts):
+        to_right, to_left = copies(c)
+        pl.when(me < n - 1)(to_right.wait_send)
+        pl.when(me > 0)(to_left.wait_send)
+    share_wait("bricks", infos, info, send, recv)
+
+
+def side_by_side(ref):
+    return jnp.concatenate([ref[s] for s in range(ref.shape[0])], axis=1)
+
+
+def unpacked(packed, frames, groups):
+    count = frames // groups
+    width = packed.shape[1] // groups
+    cuts = [packed[:count, g * width : (g + 1) * width] for g in range(groups)]
+    return jnp.concatenate(cuts, axis=0), packed[count : count + 1, :width]
+
+
+def local_kernel(
+    tiles, at, y_tiles, foot, infos, columns, message, windows, own, slot_traces
+):
+    n = lax.axis_size("bricks")
+    slots = foot.shape[0]
+    frames = y_tiles.shape[1]
     sub = lax.broadcasted_iota(jnp.int32, (slots, 2 * LANES), 0)
     mine = jnp.zeros((slots, 2 * LANES), jnp.float32)
     for k in range(slots):
@@ -381,19 +390,27 @@
     both = jnp.concatenate([component, mine])
     wanted = (both[None, :] * packs + order).reshape(packs * (slots + owned), 1).astype(f32)
 
-    low, high, infos, at = pl.pallas_call(
+    y_tiles, infos, at = pl.pallas_call(
         first_exchange,
         out_shape=(
-            sds((SWEEPS, rows, frames, width), jnp.bfloat16),
-            sds((SWEEPS, rows, frames, width), jnp.bfloat16),
+            sds((tiles, frames, LANES), jnp.bfloat16),
             sds((n,) + info.shape, f32),
             sds((slots, LANES), jnp.int32),
         ),
         in_specs=[VMEM] * 3,
-        out_specs=(VMEM,) * 4,
-        scratch_shapes=[dma((2,)), dma((2,)), dma((n,)), dma((n,))],
+        out_specs=(VMEM,) * 3,
+        scratch_shapes=[
+            pltpu.VMEM((SWEEPS, rows, frames, width), jnp.bfloat16),
+            pltpu.VMEM((SWEEPS, rows, frames, width), jnp.bfloat16),
+            pltpu.VMEM((planes + 4, rows, frames, width), f32),
+            pltpu.VMEM((planes + 2, rows, frames, width), f32),
+            dma((2, CUTS)),
+            dma((2, CUTS)),
+            dma((n,)),
+            dma((n,)),
+        ],
         compiler_params=pltpu.CompilerParams(
-            collective_id=0, has_side_effects=True, vmem_limit_bytes=16 << 20
+            collective_id=0, has_side_effects=True, vmem_limit_bytes=32 << 20
         ),
         name="first_exchange",
     )(rec, info, footprints)
@@ -406,16 +423,11 @@
             sds((slots, 2 * LANES), f32),
             sds((frames, slots), f32),
         ),
-        in_specs=[SMEM] + [VMEM] * 6,
+        in_specs=[SMEM] + [VMEM] * 4,
         out_specs=(VMEM,) * 4,
-        scratch_shapes=[
-            pltpu.VMEM((planes + 4, rows, frames, width), f32),
-            pltpu.VMEM((planes + 2, rows, frames, width), f32),
-            pltpu.VMEM((tiles, frames, LANES), jnp.bfloat16),
-        ],
         compiler_params=pltpu.CompilerParams(vmem_limit_bytes=32 << 20),
-        name="denoise_project",
-    )(at, rec, low, high, footprints, infos, columns)
+        name="project",
+    )(at, y_tiles, footprints, infos, columns)
 
     prior = jnp.concatenate([slot_traces, traces.astype(f32)], axis=1)
 

time: 50.7 us -> 47.8 us (0.943)
  Pallas kernels: 44.7 us -> 41.7 us
    pallas_call x1, Pallas kernels: 12.7 us -> 1.72 us  [shards(): pl.pallas_call(functools.partial(local_kernel, tiles), out_shape=(sds((hi...]
    pallas_call x1, Pallas kernels: 13.5 us -> 18.5 us  [shards(): pl.pallas_call(first_exchange, out_shape=(sds((tiles, frames, LANES), jnp...]
    pallas_call x1, Pallas kernels: 16.1 us -> 19 us  [shards(): pl.pallas_call(functools.partial(second_exchange, frames), out_shape=(sds...]
where the time goes in v4:
time: 47.8 us; the launch traced here: 47.5 us
  Pallas kernels  41.7 us (87%)
  local copies, waits for them, and re-layouts  3.44 us (7%)
  other arithmetic  1.66 us (3%)
  between operations  0.71 us (1%)
    pallas_call x1, Pallas kernels, shards(): pl.pallas_call(functools.partial(second_exchange, frames), out_shape=(sds...  19 us
    pallas_call x1, Pallas kernels, shards(): pl.pallas_call(first_exchange, out_shape=(sds((tiles, frames, LANES), jnp...  18.5 us
    unnamed x9, local copies, waits for them, and re-layouts  3.02 us
    pallas_call x1, Pallas kernels, shards(): pl.pallas_call(functools.partial(spread_kernel, tiles), out_shape=(sds((s...  2.45 us
    pallas_call x1, Pallas kernels, shards(): pl.pallas_call(functools.partial(local_kernel, tiles), out_shape=(sds((hi...  1.72 us

profile of v4, /device:TPU:0, one launch (start us, length us, event | category | flops | bytes accessed | tf_op | source)
XLA Modules:
  0.0 47.5 jit_solution(17736522665564885397)
XLA Ops:
  0.6 0.0 copy-start
  0.6 0.8 %broadcast_multiply_fusion = (s32[32]{0:T(128)S(1)}, s32[32]{0:T(128)S(1)}, s32[32]{0:T(128)S(1)}) fusion(s32[32]{0:T(128)} %param.9, s32[32,1]{0,1:T(1,128)} %param.8, s32[]{:T(128)S(6)} %mul.32), kind=kLoop, calls=%fused_computation.10 | loop fusion | flops 128 | bytes 644 | tf_op jit(solution)/shard_map/mul | solution.py:384
  1.4 0.1 convert_element_type.26
  1.5 0.7 %convert_element_type.24 = f32[16,32]{1,0:T(8,128)S(1)} convert(bf16[16,32]{1,0:T(8,128)(2,1)} %param.6) | non-fusion elementwise | flops 512 | bytes 3072 | tf_op jit(solution)/shard_map/convert_element_type | solution.py:383
  2.2 0.1 reshape.107
  2.3 1.3 %copy.15 = bf16[16,4,16,256]{3,0,2,1:T(8,128)(2,1)S(1)} copy(bf16[16,4,16,256]{3,2,1,0:T(8,128)(2,1)} %param.5) | data formatting | bytes 1048576 | tf_op args[0]
  3.6 0.0 copy-done
  3.6 18.5 %first_exchange.1 = (bf16[128,16,128]{2,1,0:T(8,128)(2,1)S(1)}, f32[16,8,128]{2,1,0:T(8,128)S(1)}, s32[32,128]{1,0:T(8,128)S(1)}) custom-call(bf16[4,16,16,256]{3,2,1,0:T(8,128)(2,1)S(1)} %bitcast.9, f32[8,128]{1,0:T(8,128)S(1)} %select_maximum_fusion.info, bf16[32,16384]{1,0:T(8,128)(2,1)S(1)} %copy-done), custom_call_target="tpu_custom_call" | custom-call | tf_op jit(solution)/shard_map/first_exchange/pallas_call | solution.py:393
  22.2 0.0 copy-start.1
  22.2 0.1 add.83.columns
  22.3 0.5 %copy-done.1 = s32[32,128]{1,0:T(8,128)} copy-done((s32[32,128]{1,0:T(8,128)}, s32[32,128]{1,0:T(8,128)S(1)}, u32[]{:S(2)}) %copy-start.1) | copy-done | bytes 16408
  22.8 1.7 %project.1 = (f32[8,128]{1,0:T(8,128)S(1)}, bf16[32,48,256]{2,1,0:T(8,128)(2,1)S(1)}, f32[32,256]{1,0:T(8,128)S(1)}, f32[16,32]{1,0:T(8,128)S(1)}) custom-call(s32[32,128]{1,0:T(8,128)S(1)} %get-tuple-element.13.at, bf16[128,16,128]{2,1,0:T(8,128)(2,1)S(1)} %get-tuple-element.14.y_tiles, bf16[32,16384]{1,0:T(8,128)(2,1)S(1)} %copy-done, ...), custom_call_target="tpu_custom_call" | custom-call | tf_op jit(solution)/shard_map/project/pallas_call | solution.py:418
  24.5 0.1 pad_maximum_fusion.prior
  24.6 0.1 add_multiply_fusion
  24.7 0.1 convert_element_type.29.wanted
  24.9 19.0 %second_exchange.1 = (f32[16,32]{1,0:T(8,128)S(1)}, f32[32,256]{1,0:T(8,128)S(1)}) custom-call(f32[8,128]{1,0:T(8,128)S(1)} %get-tuple-element.16.message, f32[16,8,128]{2,1,0:T(8,128)S(1)} %get-tuple-element.15.infos, f32[256,1]{1,0:T(8,128)S(1)} %convert_element_type.29.wanted, f32[16,64]{1,0:T(8,128)S(1)} %pad_maximum_fusion.prior, ...), custom_call_target="tpu_custom_call" | custom-call | tf_op jit(solution)/shard_map/second_exchange/pallas_call | solution.py:434
  43.9 0.0 copy-start.2
  43.9 0.6 %copy-done.2 = f32[32,256]{1,0:T(8,128)} copy-done((f32[32,256]{1,0:T(8,128)}, f32[32,256]{1,0:T(8,128)S(1)}, u32[]{:S(2)}) %copy-start.2) | copy-done | bytes 32792
  44.5 0.0 copy-start.3
  44.5 0.6 %copy-done.3 = f32[16,32]{1,0:T(8,128)} copy-done((f32[16,32]{1,0:T(8,128)}, f32[16,32]{1,0:T(8,128)S(1)}, u32[]{:S(2)}) %copy-start.3) | copy-done | bytes 2072
  45.1 2.5 %spread.1 = (bf16[32,16384]{1,0:T(8,128)(2,1)}, f32[16,32]{1,0:T(8,128)}) custom-call(s32[32,128]{1,0:T(8,128)} %copy-done.1, f32[32,256]{1,0:T(8,128)} %copy-done.2, f32[16,32]{1,0:T(8,128)} %copy-done.3), custom_call_target="tpu_custom_call" | custom-call | tf_op jit(solution)/shard_map/spread/pallas_call | solution.py:456
  (4 shorter events, 0.0 us)
Async XLA Ops:
  0.6 3.0 %copy-start = (bf16[32,16384]{1,0:T(8,128)(2,1)S(1)}, bf16[32,16384]{1,0:T(8,128)(2,1)}, u32[]{:S(2)}) copy-start(bf16[32,16384]{1,0:T(8,128)(2,1)} %foot.3) | copy-start | bytes 3145732
  22.2 0.6 %copy-start.1 = (s32[32,128]{1,0:T(8,128)}, s32[32,128]{1,0:T(8,128)S(1)}, u32[]{:S(2)}) copy-start(s32[32,128]{1,0:T(8,128)S(1)} %get-tuple-element.13.at) | copy-start | bytes 49156
  43.9 0.6 %copy-start.2 = (f32[32,256]{1,0:T(8,128)}, f32[32,256]{1,0:T(8,128)S(1)}, u32[]{:S(2)}) copy-start(f32[32,256]{1,0:T(8,128)S(1)} %get-tuple-element.20.result) | copy-start | bytes 98308
  44.5 0.6 %copy-start.3 = (f32[16,32]{1,0:T(8,128)}, f32[16,32]{1,0:T(8,128)S(1)}, u32[]{:S(2)}) copy-start(f32[16,32]{1,0:T(8,128)S(1)} %get-tuple-element.21.new) | copy-start | bytes 6148

commit v5 on v4

--- a/solution.py
+++ b/solution.py
@@ -9,7 +9,7 @@
 
 TIME_STEP = 0.14
 SWEEPS = 3
-CUTS = 4
+CUTS = 8
 LANES = 128
 HIGHEST = lax.Precision.HIGHEST
 MESH = pl.DeviceIdType.MESH
@@ -118,7 +118,7 @@
     planes, rows, frames, width = rec.shape
     shape = (frames, width)
     per = width // LANES
-    cuts = CUTS if rows % CUTS == 0 and rows // CUTS > SWEEPS else 1
+    cuts = CUTS if rows % CUTS == 0 else 1
     part = rows // cuts
     meet(("bricks",))
 
@@ -191,6 +191,8 @@
         pl.when(me < n - 1)(to_left.wait_recv)
         for i in range(SWEEPS):
             end = rows if c == cuts - 1 else (c + 1) * part - 1 - i
+            if end <= done[i]:
+                continue
             carried[i] = sweep(
                 loads[i], stores[i], planes + 2 * (SWEEPS - 1 - i), rows, shape, done[i], end, carried[i]
             )
@@ -278,7 +280,7 @@
 
 
 def second_exchange(
-    frames, message, infos, wanted, prior, windows, own, new_out, result,
+    frames, message, infos, wanted, prior, windows, own, result,
     gathered, same, grad, grads, send, recv, gsend, grecv,
 ):
     n = lax.axis_size("bricks")
@@ -304,7 +306,8 @@
     found = found[:high] + found[high : 2 * high] + found[2 * high :]
     summed, diag = unpacked(found, frames, LANES // slots)
     new = jnp.maximum(0.0, prior[...] + summed / (diag + 1.0))
-    new_out[...] = new[:, slots:]
+    result[:, 2 * LANES :] = jnp.zeros((slots, LANES), jnp.float32)
+    result[:frames, 2 * LANES : 2 * LANES + new.shape[1] - slots] = new[:, slots:]
     turn = lax.broadcasted_iota(jnp.int32, (slots, slots), 0) == lax.broadcasted_iota(
         jnp.int32, (slots, slots), 1
     )
@@ -347,21 +350,22 @@
         whole = whole + grads[g]
     current = own[...]
     step = whole[:, : 2 * LANES] / (whole[:, 2 * LANES : 2 * LANES + 1] + 1.0)
-    result[...] = jnp.where(current > 0, jnp.maximum(current + step, 0.0), 0.0)
-
-
-def spread_kernel(tiles, at, result, new, out, new_out):
+    result[:, : 2 * LANES] = jnp.where(current > 0, jnp.maximum(current + step, 0.0), 0.0)
+
+
+def spread_kernel(tiles, at, result, out, new_out):
     slots, width = out.shape
     base = pl.program_id(0) * (width // LANES)
     first = at[...] - base
     second = jnp.where(at[...] + 1 == tiles, 0, at[...] + 1) - base
     head = result[:, :LANES]
-    tail = result[:, LANES:]
+    tail = result[:, LANES : 2 * LANES]
     for t in range(width // LANES):
         out[:, t * LANES : (t + 1) * LANES] = jnp.where(
             first == t, head, jnp.where(second == t, tail, 0.0)
         ).astype(jnp.bfloat16)
-    new_out[...] = new[...]
+    frames, owned = new_out.shape
+    new_out[...] = result[:frames, 2 * LANES : 2 * LANES + owned]
 
 
 def shards(recording, traces, footprints, block_owner, block_slot):
@@ -431,11 +435,11 @@
 
     prior = jnp.concatenate([slot_traces, traces.astype(f32)], axis=1)
 
-    new, result = pl.pallas_call(
+    result = pl.pallas_call(
         functools.partial(second_exchange, frames),
-        out_shape=(sds((frames, owned), f32), sds((slots, 2 * LANES), f32)),
+        out_shape=sds((slots, 3 * LANES), f32),
         in_specs=[VMEM] * 6,
-        out_specs=(VMEM, VMEM),
+        out_specs=VMEM,
         scratch_shapes=[
             pltpu.VMEM((n, high_rows, LANES), f32),
             pltpu.VMEM((packs * (slots + owned), n * LANES), jnp.bfloat16),
@@ -459,15 +463,14 @@
         grid=(steps,),
         in_specs=[
             pl.BlockSpec((slots, LANES), lambda i: (0, 0)),
-            pl.BlockSpec((slots, 2 * LANES), lambda i: (0, 0)),
-            pl.BlockSpec((frames, owned), lambda i: (0, 0)),
+            pl.BlockSpec((slots, 3 * LANES), lambda i: (0, 0)),
         ],
         out_specs=(
             pl.BlockSpec((slots, voxels // steps), lambda i: (0, i)),
             pl.BlockSpec((frames, owned), lambda i: (0, 0)),
         ),
         name="spread",
-    )(at, result, new)
+    )(at, result)
     return (traces_new, footprints_new)
 
 

time: 47.8 us -> 47.2 us (0.987)
  local copies, waits for them, and re-layouts: 3.44 us -> 2.86 us
    unnamed x9 -> x7, local copies, waits for them, and re-layouts: 3.02 us -> 2.43 us
where the time goes in v5:
time: 47.2 us; the launch traced here: 46.9 us
  Pallas kernels  41.6 us (88%)
  local copies, waits for them, and re-layouts  2.86 us (6%)
  other arithmetic  1.66 us (4%)
  between operations  0.71 us (2%)
    pallas_call x1, Pallas kernels, shards(): pl.pallas_call(functools.partial(second_exchange, frames), out_shape=sds(...  18.8 us
    pallas_call x1, Pallas kernels, shards(): pl.pallas_call(first_exchange, out_shape=(sds((tiles, frames, LANES), jnp...  18.6 us
    pallas_call x1, Pallas kernels, shards(): pl.pallas_call(functools.partial(spread_kernel, tiles), out_shape=(sds((s...  2.51 us
    unnamed x7, local copies, waits for them, and re-layouts  2.43 us
    pallas_call x1, Pallas kernels, shards(): pl.pallas_call(functools.partial(local_kernel, tiles), out_shape=(sds((hi...  1.72 us

profile of v5, /device:TPU:0, one launch (start us, length us, event | category | flops | bytes accessed | tf_op | source)
XLA Modules:
  0.0 46.9 jit_solution(699667937367275853)
XLA Ops:
  0.6 0.0 copy-start
  0.6 0.8 %broadcast_multiply_fusion = (s32[32]{0:T(128)S(1)}, s32[32]{0:T(128)S(1)}, s32[32]{0:T(128)S(1)}) fusion(s32[32]{0:T(128)} %param.9, s32[32,1]{0,1:T(1,128)} %param.8, s32[]{:T(128)S(6)} %mul.32), kind=kLoop, calls=%fused_computation.10 | loop fusion | flops 128 | bytes 644 | tf_op jit(solution)/shard_map/mul | solution.py:388
  1.4 0.1 convert_element_type.26
  1.5 0.7 %convert_element_type.24 = f32[16,32]{1,0:T(8,128)S(1)} convert(bf16[16,32]{1,0:T(8,128)(2,1)} %param.6) | non-fusion elementwise | flops 512 | bytes 3072 | tf_op jit(solution)/shard_map/convert_element_type | solution.py:387
  2.2 0.1 reshape.107
  2.3 1.3 %copy.15 = bf16[16,4,16,256]{3,0,2,1:T(8,128)(2,1)S(1)} copy(bf16[16,4,16,256]{3,2,1,0:T(8,128)(2,1)} %param.5) | data formatting | bytes 1048576 | tf_op args[0]
  3.6 0.0 copy-done
  3.6 18.6 %first_exchange.1 = (bf16[128,16,128]{2,1,0:T(8,128)(2,1)S(1)}, f32[16,8,128]{2,1,0:T(8,128)S(1)}, s32[32,128]{1,0:T(8,128)S(1)}) custom-call(bf16[4,16,16,256]{3,2,1,0:T(8,128)(2,1)S(1)} %bitcast.9, f32[8,128]{1,0:T(8,128)S(1)} %select_maximum_fusion.info, bf16[32,16384]{1,0:T(8,128)(2,1)S(1)} %copy-done), custom_call_target="tpu_custom_call" | custom-call | tf_op jit(solution)/shard_map/first_exchange/pallas_call | solution.py:397
  22.3 0.0 copy-start.2
  22.3 0.1 add.83.columns
  22.4 0.5 %copy-done.2 = s32[32,128]{1,0:T(8,128)} copy-done((s32[32,128]{1,0:T(8,128)}, s32[32,128]{1,0:T(8,128)S(1)}, u32[]{:S(2)}) %copy-start.2) | copy-done | bytes 16408
  22.9 1.7 %project.1 = (f32[8,128]{1,0:T(8,128)S(1)}, bf16[32,48,256]{2,1,0:T(8,128)(2,1)S(1)}, f32[32,256]{1,0:T(8,128)S(1)}, f32[16,32]{1,0:T(8,128)S(1)}) custom-call(s32[32,128]{1,0:T(8,128)S(1)} %get-tuple-element.11.at, bf16[128,16,128]{2,1,0:T(8,128)(2,1)S(1)} %get-tuple-element.12.y_tiles, bf16[32,16384]{1,0:T(8,128)(2,1)S(1)} %copy-done, ...), custom_call_target="tpu_custom_call" | custom-call | tf_op jit(solution)/shard_map/project/pallas_call | solution.py:422
  24.6 0.1 pad_maximum_fusion.prior
  24.7 0.1 add_multiply_fusion
  24.8 0.1 convert_element_type.29.wanted
  25.0 18.8 %second_exchange.1.result = f32[32,384]{1,0:T(8,128)S(1)} custom-call(f32[8,128]{1,0:T(8,128)S(1)} %get-tuple-element.14.message, f32[16,8,128]{2,1,0:T(8,128)S(1)} %get-tuple-element.13.infos, f32[256,1]{1,0:T(8,128)S(1)} %convert_element_type.29.wanted, f32[16,64]{1,0:T(8,128)S(1)} %pad_maximum_fusion.prior, ...), custom_call_target="tpu_custom_call" | custom-call | tf_op jit(solution)/shard_map/second_exchange/pallas_call | solution.py:438
  43.8 0.0 copy-start.1
  43.8 0.6 %copy-done.1 = f32[32,384]{1,0:T(8,128)} copy-done((f32[32,384]{1,0:T(8,128)}, f32[32,384]{1,0:T(8,128)S(1)}, u32[]{:S(2)}) %copy-start.1) | copy-done | bytes 49176
  44.4 2.5 %spread.1 = (bf16[32,16384]{1,0:T(8,128)(2,1)}, f32[16,32]{1,0:T(8,128)}) custom-call(s32[32,128]{1,0:T(8,128)} %copy-done.2, f32[32,384]{1,0:T(8,128)} %copy-done.1), custom_call_target="tpu_custom_call" | custom-call | tf_op jit(solution)/shard_map/spread/pallas_call | solution.py:460
  (4 shorter events, 0.0 us)
Async XLA Ops:
  0.6 3.0 %copy-start = (bf16[32,16384]{1,0:T(8,128)(2,1)S(1)}, bf16[32,16384]{1,0:T(8,128)(2,1)}, u32[]{:S(2)}) copy-start(bf16[32,16384]{1,0:T(8,128)(2,1)} %foot.3) | copy-start | bytes 3145732
  22.3 0.6 %copy-start.2 = (s32[32,128]{1,0:T(8,128)}, s32[32,128]{1,0:T(8,128)S(1)}, u32[]{:S(2)}) copy-start(s32[32,128]{1,0:T(8,128)S(1)} %get-tuple-element.11.at) | copy-start | bytes 49156
  43.8 0.6 %copy-start.1 = (f32[32,384]{1,0:T(8,128)}, f32[32,384]{1,0:T(8,128)S(1)}, u32[]{:S(2)}) copy-start(f32[32,384]{1,0:T(8,128)S(1)} %second_exchange.1.result) | copy-start | bytes 147460
